TPU v7x, 256 devices: a whole 4x4x8 slice. The times are simulated.
256 devices in a mesh: row: 16 (over x, z_hi), col: 8 (over z_lo, y), snode: 2 (over core).
Axes of the slice: x: 4, y: 4, z: 8 (z_hi: 4, z_lo: 2; z = z_hi * 2 + z_lo), core: 2. Of those that a mesh axis runs over, the one named last changes fastest.
Arguments:
- ancestor_inverse: bfloat16 [40960, 20480], P(('snode', 'row'), 'col'), parts along dimension 0, may hold values from -8 to 8
- fill_mask: int32 [160, 80], P('snode'), parts along dimension 0, may hold values from 0 to 1, as said below
- block_order: int32 [4, 80], P('snode'), parts along dimension 0, may hold values from 0 to 79, each once within a row
- l_rows: bfloat16 [4, 20480, 256], P('snode', ('row', 'col')), parts along dimension 0, may hold values from -6 to 6
- diag_inverse: bfloat16 [4, 256, 256], P('snode'), parts along dimension 0, may hold values from -0.0024414062 to 0.0024414062
Outputs:
- ainv_kr: bfloat16 [4, 256, 20480], P('snode', None, ('row', 'col')), parts along dimension 0
There are 2 independent parts, one for each index of `snode`. A program takes and returns all parts, laid end to end along the dimension named above; each array names one. Nothing has to cross between parts.
Inputs may be any that keep to these rules, and one draw needn't show every extreme that they name: Tile (i, j) takes part exactly where fill_mask is 1; diagonal tiles are always 1. `block_order`: each row is a permutation of the 80 ancestor blocks.
All inputs are finite; a program needn't handle non-finite values.
Results may differ from a plain program's by a relative error of at most 0.014.
Values may be sent and summed in bfloat16 or wider, within the bound.
No kernel may reach another device: no remote copies, remote signals or barrier semaphores. Data moves between devices by JAX's collectives and lax.ppermute only.
A program may use at most 128 MiB of HBM per device.

v0:
```python
import jax
import jax.numpy as jnp
from jax import lax
from jax.sharding import PartitionSpec as P


def per_device(ancestor_inverse, fill_mask, block_order, l_rows, diag_inverse):
    row_index = lax.axis_index("row")
    col_index = lax.axis_index("col")
    local_rows = ancestor_inverse.shape[0]
    local_cols = ancestor_inverse.shape[1]
    snode_count = diag_inverse.shape[0]
    tile_size = diag_inverse.shape[1]
    block_count = fill_mask.shape[0]
    row_blocks = local_rows // tile_size
    col_blocks = local_cols // tile_size
    normed = jnp.einsum(
        "sxy,syz->sxz", l_rows, diag_inverse, preferred_element_type=jnp.float32
    ).astype(jnp.bfloat16)
    wanted = col_index * col_blocks + jnp.arange(col_blocks, dtype=jnp.int32)
    everything = lax.all_gather(normed, ("row", "col"), axis=1, tiled=True)
    pieces = everything.reshape(snode_count, block_count, tile_size, tile_size)
    selector = (block_order[:, None, :] == wanted[None, :, None]).astype(jnp.bfloat16)
    columns = jnp.einsum(
        "saq,sqxy->saxy", selector, pieces, preferred_element_type=jnp.float32
    ).astype(jnp.bfloat16)
    stacked = columns.transpose(1, 2, 0, 3).reshape(local_cols, snode_count * tile_size)
    tile_gate = lax.dynamic_slice(
        fill_mask, (row_index * row_blocks, col_index * col_blocks), (row_blocks, col_blocks)
    ).astype(jnp.bfloat16)
    masked = (
        ancestor_inverse.reshape(row_blocks, tile_size, col_blocks, tile_size)
        * tile_gate[:, None, :, None]
    ).reshape(local_rows, local_cols)
    share_rows = local_rows // lax.axis_size("col")
    partial_value = -jnp.dot(masked, stacked, preferred_element_type=jnp.float32)
    summed = lax.psum(partial_value.astype(jnp.bfloat16), "col").astype(jnp.float32)
    own_rows = lax.dynamic_slice_in_dim(summed, col_index * share_rows, share_rows, 0)
    return (
        own_rows.reshape(share_rows, snode_count, tile_size).transpose(1, 2, 0).astype(jnp.bfloat16)
    )


def solution(mesh):
    return jax.shard_map(
        per_device,
        mesh=mesh,
        in_specs=(
            P(("snode", "row"), "col"),
            P("snode", None),
            P("snode", None),
            P("snode", ("row", "col"), None),
            P("snode", None, None),
        ),
        out_specs=P("snode", None, ("row", "col")),
        check_vma=False,
    )
```

profile of v0, /device:TPU:32, one launch (start us, length us, event | category | flops | bytes accessed | tf_op | source)
XLA Modules:
  0.0 297.8 jit_solution(8407568117933270952)
XLA Ops:
  6.5 0.0 copy-start
  6.5 0.0 all-gather.2.cloned.1.call-start
  6.5 0.9 copy-done
  7.5 1.8 convolution_convert_fusion
  9.3 0.0 all-gather.2.cloned.1.call-update
  9.3 0.0 all-reduce.2.cloned.1.call-start
  9.4 0.8 dynamic-slice_convert_fusion
  10.1 4.7 %mul.23 = bf16[5,256,10,256]{3,2,1,0:T(8,128)(2,1)} broadcast(bf16[5,10]{1,0:T(8,128)(2,1)S(1)} %dynamic-slice_convert_fusion), dimensions={0,2} | broadcast | bytes 6553700 | tf_op jit(solution)/shard_map/mul | solution.py:32
  14.8 0.0 copy-start.2
  14.8 11.2 %copy.13 = bf16[160,8,10,256]{3,1,2,0:T(8,128)(2,1)} copy(bf16[160,8,10,256]{3,2,1,0:T(8,128)(2,1)} %bitcast.24) | data formatting | bytes 13107200
  26.0 150.5 %all-gather.2.cloned.1.call-done = bf16[2,20480,256]{2,1,0:T(8,128)(2,1)} async-done(((bf16[2,160,256]{2,1,0:T(8,128)(2,1)}), bf16[2,20480,256]{2,1,0:T(8,128)(2,1)}) %all-gather.2.cloned.1.call-update) | async-done | bytes 20971536 | tf_op jit(solution)/shard_map/all_gather | solution.py:21
  176.6 0.0 copy-done.2
  176.6 20.5 %convert_bitcast_fusion = bf16[10,256,2,256]{3,0,1,2:T(8,128)(2,1)S(1)} fusion(bf16[2,80,256,256]{3,2,1,0:T(8,128)(2,1)} %bitcast.25, s32[2,80]{1,0:T(2,128)S(1)} %copy-done.2, s32[10]{0:T(128)S(1)} %iota_add_fusion), kind=kOutput, calls=%fused_computation.4 | convolution fusion | flops 211027520 | bytes 23593640 | tf_op jit(solution)/shard_map/saq,sqxy->saxy/dot_general | solution.py:24
  197.1 0.0 copy-start.1
  197.1 2.7 copy.9
  199.8 0.5 copy.14
  200.3 0.0 copy-done.1
  200.3 7.6 %fusion.7 = bf16[1280,512]{1,0:T(8,128)(2,1)} fusion(bf16[2560,512]{1,0:T(8,128)(2,1)S(1)} %bitcast.28, bf16[1280,2560]{1,0:T(8,128)(2,1)} %param.5, bf16[1280,2560]{1,0:T(8,128)(2,1)S(1)} %bitcast.27), kind=kOutput, calls=%fused_computation.6 | convolution fusion | flops 3360030720 | bytes 17039360 | tf_op jit(solution)/shard_map/dot_general | solution.py:36
  207.9 0.0 all-reduce.2.cloned.1.call-update
  207.9 81.4 %all-reduce.2.cloned.1.call-done = bf16[1280,512]{1,0:T(8,128)(2,1)} async-done(((bf16[1280,512]{1,0:T(8,128)(2,1)}), bf16[1280,512]{1,0:T(8,128)(2,1)}) %all-reduce.2.cloned.1.call-update) | async-done | bytes 1310736 | tf_op jit(solution)/shard_map/psum | solution.py:37
  289.3 0.9 convert_convert_fusion
  290.3 0.7 copy.20
  (1 shorter events, 0.0 us)
Async XLA Ops:
  6.5 1.0 copy-start
  6.5 170.0 %all-gather.2.cloned.1.call-start = ((), (), s32[]{:S(2)}) async-start(), calls=%async_computation | async-start | bytes 21135360 | tf_op jit(solution)/shard_map/all_gather | solution.py:21
  9.3 280.0 %all-reduce.2.cloned.1.call-start = ((), (), s32[]{:S(2)}) async-start(), calls=%async_computation.1 | async-start | bytes 2621440 | tf_op jit(solution)/shard_map/psum | solution.py:37
  14.8 161.7 %copy-start.2 = (s32[2,80]{1,0:T(2,128)S(1)}, s32[2,80]{1,0:T(2,128)}, u32[]{:S(2)}) copy-start(s32[2,80]{1,0:T(2,128)} %param.7) | copy-start | bytes 1924
  197.1 3.2 %copy-start.1 = (bf16[160,8,10,256]{3,1,2,0:T(8,128)(2,1)S(1)}, bf16[160,8,10,256]{3,1,2,0:T(8,128)(2,1)}, u32[]{:S(2)}) copy-start(bf16[160,8,10,256]{3,1,2,0:T(8,128)(2,1)} %copy.13) | copy-start | bytes 19660804
Sparse Core Ops, SparseCore 0:
  10.9 165.6 all-gather.1
  208.0 81.2 all-reduce.1
where the time goes:
time: 299 us; the launch traced here: 298 us
  waiting for transfers between devices  232 us (78%)
  matrix products  29.9 us (10%)
  local copies, waits for them, and re-layouts  20.7 us (7%)
  between operations  13.5 us (5%)
    all_gather x1, waiting for transfers between devices, per_device(): everything = lax.all_gather(normed, ('row', 'col'), axis=1, tiled=True)  151 us
    psum x1, waiting for transfers between devices, per_device(): lax.psum(partial_value.astype(jnp.bfloat16), 'col').astype(jnp.float32)  81.4 us
    dot_general x1, matrix products, per_device(): jnp.einsum('saq,sqxy->saxy', selector, pieces, preferred_element_type=jnp...  20.5 us
    unnamed x8, local copies, waits for them, and re-layouts  12.6 us
    dot_general x1, matrix products, per_device(): jnp.dot(masked, stacked, preferred_element_type=jnp.float32)  7.58 us
  transfers between devices with their start and end apart: 2, of which 2 were waited for; matrix products, arithmetic and copies ran while one was open for 6% of the time, Pallas kernels for 0%

commit v1 on v0

v1 whole, which is shorter than its diff:
```python
import functools

import jax
import jax.numpy as jnp
from jax import lax
from jax.experimental import pallas as pl
from jax.experimental.pallas import tpu as pltpu
from jax.sharding import PartitionSpec as P

NX, NZ = 4, 4
VMEM = pltpu.VMEM
SMEM = pltpu.SMEM
SLICE = 16


def whole(space=VMEM):
    return pl.BlockSpec(memory_space=space)


def params():
    return pltpu.CompilerParams(vmem_limit_bytes=48 * 1024 * 1024)


def spread_kernel(pos_ref, l_ref, out_ref):
    rows = out_ref.shape[0]
    first = pos_ref[0] + pos_ref[1] * (l_ref.shape[1] // SLICE)
    for i in range(l_ref.shape[1] // SLICE):
        slot = lax.rem(first + i, rows)
        for s in range(l_ref.shape[0]):
            out_ref[slot, s] = l_ref[s, i * SLICE : (i + 1) * SLICE]


def compact_kernel(pos_ref, got_ref, out_ref):
    rows = got_ref.shape[0]
    count = out_ref.shape[1]
    first = pos_ref[0] - pos_ref[1] * count + 16 * rows
    for i in range(count):
        slot = lax.rem(first - i, rows)
        for copy in range(out_ref.shape[0]):
            out_ref[copy, i] = got_ref[slot]


def select_kernel(pos_ref, order_ref, all_ref, diag_ref, out_ref, from_ref, picked):
    snodes, blocks = order_ref.shape
    rows = 16
    per_row = blocks // rows
    share = out_ref.shape[0] // SLICE
    tile = diag_ref.shape[1]

    def step(q, carry):
        group = q // per_row
        k = lax.rem(pos_ref[0] - group + rows, rows)
        place = (q - group * per_row) * rows + k
        for s in range(snodes):
            a = order_ref[s, q] - pos_ref[1] * share

            @pl.when((a >= 0) & (a < share))
            def _():
                picked[s, pl.ds(pl.multiple_of(a * SLICE, SLICE), SLICE), :] = all_ref[place, s]
                from_ref[s, a] = group

        return carry

    lax.fori_loop(0, blocks, step, 0)
    for s in range(snodes):
        out_ref[:, s * tile : (s + 1) * tile] = jnp.dot(
            picked[s], diag_ref[s], preferred_element_type=jnp.float32
        ).astype(out_ref.dtype)


def product_kernel(pos_ref, from_ref, mask_ref, a_ref, o_ref, u_ref, d_ref, fu_ref, fd_ref, out_ref, stacked, *, zshift):
    i = pl.program_id(0)
    rows = 16
    share = stacked.shape[0] // (rows * SLICE)
    tile = rows * SLICE
    x, z = pos_ref[2], pos_ref[3]
    block = share * SLICE

    @pl.when(i == 0)
    def _():
        pieces = []
        for xs, ref, base in ((0, o_ref, 0), (-1, u_ref, 0), (1, d_ref, 0)):
            for n, zs in enumerate(zshift):
                pieces.append((xs, zs, ref, n * block))
        half = len(zshift) // 2
        for n, zs in enumerate(zshift):
            pieces.append((2, zs, fu_ref, n * block) if n < half else (2, zs, fd_ref, (n - half) * block))
        for s in range(from_ref.shape[0]):
            for a in range(share):
                group = from_ref[s, a]
                for xs, zs, ref, base in pieces:
                    j = lax.rem(x + xs + NX, NX) * NZ + lax.rem(z + zs + NZ, NZ)
                    k = lax.rem(j - group + rows, rows)
                    stacked[
                        pl.ds(pl.multiple_of(a * tile + k * SLICE, SLICE), SLICE), s * tile : (s + 1) * tile
                    ] = ref[base + a * SLICE : base + (a + 1) * SLICE, s * tile : (s + 1) * tile]

    gates = []
    for j in range(share):
        gate = mask_ref[pos_ref[0] * pl.num_programs(0) + i, pos_ref[1] * share + j]
        keep = jnp.full((1, tile), gate, jnp.int32).astype(jnp.float32)
        gates.append(keep.astype(jnp.bfloat16))
    gate_row = jnp.concatenate(gates, axis=1)
    out_ref[...] = (
        -jnp.dot(a_ref[...] * gate_row, stacked[...], preferred_element_type=jnp.float32)
    ).astype(out_ref.dtype)


def ring(value, axis, up, down):
    half = value.shape[0] // 2
    from_up = lax.ppermute(value, axis, up)
    from_down = lax.ppermute(value, axis, down)
    far_up = lax.ppermute(from_up[:half], axis, up)
    far_down = lax.ppermute(from_down[half:], axis, down)
    return from_up, from_down, far_up, far_down


def per_device(ancestor_inverse, fill_mask, block_order, l_rows, diag_inverse):
    rows, cols = lax.axis_size("row"), lax.axis_size("col")
    row_index, col_index = lax.axis_index("row"), lax.axis_index("col")
    snodes, tile = diag_inverse.shape[0], diag_inverse.shape[1]
    local_rows, local_cols = ancestor_inverse.shape
    count = l_rows.shape[1] // SLICE
    blocks = block_order.shape[1]
    share = blocks // cols
    bf16 = jnp.bfloat16
    pos = jnp.stack([row_index, col_index, row_index // NZ, row_index % NZ]).astype(jnp.int32)

    spread = pl.pallas_call(
        spread_kernel,
        out_shape=jax.ShapeDtypeStruct((rows, snodes, SLICE, tile), bf16),
        in_specs=[whole(SMEM), whole()],
        out_specs=whole(),
        compiler_params=params(),
        name="spread",
    )(pos, l_rows)
    got = lax.all_to_all(spread, "row", 0, 0, tiled=True)
    copies = pl.pallas_call(
        compact_kernel,
        out_shape=jax.ShapeDtypeStruct((cols, count, snodes, SLICE, tile), bf16),
        in_specs=[whole(SMEM), whole()],
        out_specs=whole(),
        compiler_params=params(),
        name="compact",
    )(pos, got)
    everything = lax.all_to_all(copies, "col", 0, 0, tiled=True)
    everything = everything.reshape(cols * count, snodes, SLICE, tile)
    own, source = pl.pallas_call(
        select_kernel,
        out_shape=(
            jax.ShapeDtypeStruct((share * SLICE, snodes * tile), bf16),
            jax.ShapeDtypeStruct((snodes, share), jnp.int32),
        ),
        in_specs=[whole(SMEM), whole(SMEM), whole(), whole()],
        out_specs=(whole(), whole(SMEM)),
        scratch_shapes=[VMEM((snodes, share * SLICE, tile), bf16)],
        compiler_params=params(),
        name="select",
    )(pos, block_order, everything, diag_inverse)

    def shift(dx, dz):
        return [(r, ((r // NZ + dx) % NX) * NZ + (r % NZ + dz) % NZ) for r in range(rows)]

    up, down, far_up, far_down = ring(own, "row", shift(0, 1), shift(0, -1))
    plane = jnp.concatenate([own, up, down, far_up, far_down], axis=0)
    xu, xd, xfu, xfd = ring(plane, "row", shift(1, 0), shift(-1, 0))

    row_blocks = local_rows // tile
    partial_value = pl.pallas_call(
        functools.partial(product_kernel, zshift=(0, -1, 1, 2)),
        out_shape=jax.ShapeDtypeStruct((local_rows, snodes * tile), bf16),
        grid=(row_blocks,),
        in_specs=[whole(SMEM), whole(SMEM), whole(SMEM), pl.BlockSpec((tile, local_cols), lambda i: (i, 0))]
        + [whole()] * 5,
        out_specs=pl.BlockSpec((tile, snodes * tile), lambda i: (i, 0)),
        scratch_shapes=[VMEM((local_cols, snodes * tile), bf16)],
        compiler_params=params(),
        name="product",
    )(pos, source, fill_mask, ancestor_inverse, plane, xu, xd, xfu, xfd)

    share_rows = local_rows // cols
    shares = lax.all_to_all(partial_value, "col", 0, 0, tiled=True)
    summed = shares.reshape(cols, share_rows, snodes, tile).astype(jnp.float32).sum(0)
    return summed.transpose(1, 2, 0).astype(bf16)


def solution(mesh):
    return jax.shard_map(
        per_device,
        mesh=mesh,
        in_specs=(
            P(("snode", "row"), "col"),
            P("snode", None),
            P("snode", None),
            P("snode", ("row", "col"), None),
            P("snode", None, None),
        ),
        out_specs=P("snode", None, ("row", "col")),
        check_vma=False,
    )
```

time: 299 us -> 119 us (0.40)
  waiting for transfers between devices: 232 us -> 30.2 us
  blocking collectives: 0 us -> 62.5 us
  matrix products: 29.9 us -> 0 us
  local copies, waits for them, and re-layouts: 20.7 us -> 1.77 us
  between operations: 13.5 us -> 0.13 us
  Pallas kernels: 0 us -> 12.9 us
  starting transfers between devices: 0.04 us -> 10.6 us
    all_gather x1 -> x0, waiting for transfers between devices: 151 us -> none  [per_device(): everything = lax.all_gather(normed, ('row', 'col'), axis=1, tiled=True)]
    psum x1 -> x0, waiting for transfers between devices: 81.4 us -> none  [per_device(): lax.psum(partial_value.astype(jnp.bfloat16), 'col').astype(jnp.float32)]
    all_to_all x0 -> x3, blocking collectives: none -> 62.5 us  [the longest x1 23.3 us: per_device(): got = lax.all_to_all(spread, 'row', 0, 0, tiled=True)]
    ppermute x0 -> x8, waiting for transfers between devices: none -> 30.2 us  [the longest x2 18.1 us: ring(): from_down = lax.ppermute(value, axis, down)]
    dot_general x3 -> x0, matrix products: 29.9 us -> none  [the longest x1 20.5 us: per_device(): jnp.einsum('saq,sqxy->saxy', selector, pieces, preferred_element_type=jnp...]
    pallas_call x0 -> x4, Pallas kernels: none -> 12.9 us  [the longest x1 7.94 us: per_device(): pl.pallas_call(functools.partial(product_kernel, zshift=(0, -1, 1, 2)), o...]
    unnamed x8 -> x12, local copies, waits for them, and re-layouts: 12.6 us -> 0.98 us
    ppermute x0 -> x8, starting transfers between devices: none -> 10.6 us  [the longest x2 3.91 us: ring(): from_up = lax.ppermute(value, axis, up)]
  transfers between devices with their start and end apart: 2 -> 8, of which waited for: 2 -> 5; matrix products, arithmetic and copies ran while one was open for 6% -> 0% of each run, Pallas kernels for 0% -> 0%
where the time goes in v1:
time: 119 us; the launch traced here: 118 us
  blocking collectives  62.5 us (53%)
  waiting for transfers between devices  30.2 us (25%)
  Pallas kernels  12.9 us (11%)
  starting transfers between devices  10.6 us (9%)
  local copies, waits for them, and re-layouts  1.77 us (1%)
    all_to_all x1, blocking collectives, per_device(): got = lax.all_to_all(spread, 'row', 0, 0, tiled=True)  23.3 us
    all_to_all x1, blocking collectives, per_device(): everything = lax.all_to_all(copies, 'col', 0, 0, tiled=True)  21.6 us
    ppermute x2, waiting for transfers between devices, ring(): from_down = lax.ppermute(value, axis, down)  18.1 us
    all_to_all x1, blocking collectives, per_device(): shares = lax.all_to_all(partial_value, 'col', 0, 0, tiled=True)  17.6 us
    pallas_call x1, Pallas kernels, per_device(): pl.pallas_call(functools.partial(product_kernel, zshift=(0, -1, 1, 2)), o...  7.94 us
    ppermute x2, waiting for transfers between devices, ring(): far_up = lax.ppermute(from_up[:half], axis, up)  7.49 us
    ppermute x2, waiting for transfers between devices, ring(): far_down = lax.ppermute(from_down[half:], axis, down)  4.62 us
    ppermute x2, starting transfers between devices, ring(): from_up = lax.ppermute(value, axis, up)  3.91 us
  transfers between devices with their start and end apart: 8, of which 5 were waited for; matrix products, arithmetic and copies ran while one was open for 0% of the time, Pallas kernels for 0%

profile of v1, /device:TPU:32, one launch (start us, length us, event | category | flops | bytes accessed | tf_op | source)
XLA Modules:
  0.0 118.3 jit_solution(140571082712969067)
XLA Ops:
  0.0 0.1 pad_add_fusion.pos_ref
  0.1 0.0 copy-start.1
  0.1 0.9 copy-done.1
  1.0 0.6 spread.1
  1.6 23.3 %all_to_all.19.got_ref = bf16[16,2,16,256]{3,2,1,0:T(8,128)(2,1)S(1)} all-to-all(bf16[16,2,16,256]{3,2,1,0:T(8,128)(2,1)S(1)} %spread.1), channel_id=1, replica_groups=mesh['row'=16,'col'=8,'snode'=2] {'row'}, dimensions={0} | all-to-all | bytes 524288 | tf_op jit(solution)/shard_map/all_to_all | solution.py:137
  24.8 0.6 compact.1
  25.5 0.0 copy-start
  25.5 0.0 copy-start.3
  25.5 21.6 %all_to_all.20 = bf16[8,10,2,16,256]{4,3,2,1,0:T(8,128)(2,1)S(1)} all-to-all(bf16[8,10,2,16,256]{4,3,2,1,0:T(8,128)(2,1)S(1)} %compact.1), channel_id=1, replica_groups=mesh['row'=16,'col'=8,'snode'=2] {'col'}, dimensions={0} | all-to-all | bytes 2621440 | tf_op jit(solution)/shard_map/all_to_all | solution.py:146
  47.1 0.0 copy-done
  47.1 0.0 copy-done.3
  47.1 3.7 %select.7 = (bf16[160,512]{1,0:T(8,128)(2,1)S(1)}, s32[2,10]{1,0:T(2,128)S(1)}) custom-call(s32[4]{0:T(128)S(1)} %pad_add_fusion.pos_ref, s32[2,80]{1,0:T(2,128)S(1)} %copy-done.3, bf16[80,2,16,256]{3,2,1,0:T(8,128)(2,1)S(1)} %bitcast.8, bf16[2,256,256]{2,1,0:T(8,128)(2,1)S(1)} %copy-done), custom_call_target="tpu_custom_call" | custom-call | tf_op jit(solution)/shard_map/select/pallas_call | solution.py:148
  50.8 0.1 collective-permute-start.1
  50.9 2.9 %collective-permute-start = (bf16[160,512]{1,0:T(8,128)(2,1)S(1)}, bf16[160,512]{1,0:T(8,128)(2,1)S(1)}, u32[]{:S(2)}, u32[]{:S(2)}) collective-permute-start(bf16[160,512]{1,0:T(8,128)(2,1)S(1)} %get-tuple-element.8), channel_id=1, source_target_pairs={{0,16},{16,32},{32,48},{48,0},{64,80},{80,96},{96,112},{112,64},{1... | collective-permute-start | bytes 491528 | tf_op jit(solution)/shard_map/ppermute | solution.py:111
  53.8 0.0 copy-start.2
  53.8 6.6 %collective-permute-done.1 = bf16[160,512]{1,0:T(8,128)(2,1)S(1)} collective-permute-done((bf16[160,512]{1,0:T(8,128)(2,1)S(1)}, bf16[160,512]{1,0:T(8,128)(2,1)S(1)}, u32[]{:S(2)}, u32[]{:S(2)}) %collective-permute-start.1) | collective-permute-done | bytes 163872 | tf_op jit(solution)/shard_map/ppermute | solution.py:112
  60.5 0.1 collective-permute-start.3
  60.6 0.0 collective-permute-done
  60.6 2.9 %collective-permute-start.2 = (bf16[80,512]{1,0:T(8,128)(2,1)S(1)}, bf16[80,512]{1,0:T(8,128)(2,1)S(1)}, u32[]{:S(2)}, u32[]{:S(2)}) collective-permute-start(bf16[80,512]{1,0:T(8,128)(2,1)S(1)} %slice.16), channel_id=1, source_target_pairs={{0,16},{16,32},{32,48},{48,0},{64,80},{80,96},{96,112},{112,64},{1... | collective-permute-start | bytes 245768 | tf_op jit(solution)/shard_map/ppermute | solution.py:113
  63.5 3.8 %collective-permute-done.2 = bf16[80,512]{1,0:T(8,128)(2,1)S(1)} collective-permute-done((bf16[80,512]{1,0:T(8,128)(2,1)S(1)}, bf16[80,512]{1,0:T(8,128)(2,1)S(1)}, u32[]{:S(2)}, u32[]{:S(2)}) %collective-permute-start.2) | collective-permute-done | bytes 81952 | tf_op jit(solution)/shard_map/ppermute | solution.py:113
  67.4 0.0 collective-permute-done.3
  67.4 1.1 collective-permute-start.5
  68.5 1.0 collective-permute-start.4
  69.5 11.5 %collective-permute-done.5.d_ref = bf16[640,512]{1,0:T(8,128)(2,1)S(1)} collective-permute-done((bf16[640,512]{1,0:T(8,128)(2,1)S(1)}, bf16[640,512]{1,0:T(8,128)(2,1)S(1)}, u32[]{:S(2)}, u32[]{:S(2)}) %collective-permute-start.5) | collective-permute-done | bytes 655392 | tf_op jit(solution)/shard_map/ppermute | solution.py:112
  81.0 2.4 %collective-permute-start.7 = (bf16[320,512]{1,0:T(8,128)(2,1)S(1)}, bf16[320,512]{1,0:T(8,128)(2,1)S(1)}, u32[]{:S(2)}, u32[]{:S(2)}) collective-permute-start(bf16[320,512]{1,0:T(8,128)(2,1)S(1)} %slice.19), channel_id=1, source_target_pairs={{0,192},{16,208},{32,224},{48,240},{64,0},{80,16},{96,32},{112,48}... | collective-permute-start | bytes 983048 | tf_op jit(solution)/shard_map/ppermute | solution.py:114
  83.4 0.0 collective-permute-done.4.u_ref
  83.4 0.1 collective-permute-start.6
  83.5 4.6 %collective-permute-done.7.fd_ref = bf16[320,512]{1,0:T(8,128)(2,1)S(1)} collective-permute-done((bf16[320,512]{1,0:T(8,128)(2,1)S(1)}, bf16[320,512]{1,0:T(8,128)(2,1)S(1)}, u32[]{:S(2)}, u32[]{:S(2)}) %collective-permute-start.7) | collective-permute-done | bytes 327712 | tf_op jit(solution)/shard_map/ppermute | solution.py:114
  88.1 3.7 %collective-permute-done.6.fu_ref = bf16[320,512]{1,0:T(8,128)(2,1)S(1)} collective-permute-done((bf16[320,512]{1,0:T(8,128)(2,1)S(1)}, bf16[320,512]{1,0:T(8,128)(2,1)S(1)}, u32[]{:S(2)}, u32[]{:S(2)}) %collective-permute-start.6) | collective-permute-done | bytes 327712 | tf_op jit(solution)/shard_map/ppermute | solution.py:113
  91.8 0.0 copy-done.2
  91.8 7.9 %product.1 = bf16[1280,512]{1,0:T(8,128)(2,1)S(1)} custom-call(s32[4]{0:T(128)S(1)} %pad_add_fusion.pos_ref, s32[2,10]{1,0:T(2,128)S(1)} %get-tuple-element.7.from_ref, s32[80,80]{1,0:T(8,128)S(1)} %copy-done.2, bf16[1280,2560]{1,0:T(8,128)(2,1)} %a_ref.1, bf16[640,512]{1,0:T(8,128)(2,1)S(1)} %constant_dynamic-update-slice_fusion.o_ref, ...), custom_call_target="tpu_custom_call" | custom-call | tf_op jit(solution)/shard_map/product/pallas_call | solution.py:169
  99.7 17.6 %all_to_all.21 = bf16[8,160,512]{2,1,0:T(8,128)(2,1)S(1)} all-to-all(bf16[8,160,512]{2,1,0:T(8,128)(2,1)S(1)} %bitcast.7), channel_id=1, replica_groups=mesh['row'=16,'col'=8,'snode'=2] {'col'}, dimensions={0} | all-to-all | bytes 2621440 | tf_op jit(solution)/shard_map/all_to_all | solution.py:182
  117.4 0.2 reduce_sum.12
  117.6 0.7 copy.6
  (10 shorter events, 0.2 us)
Async XLA Ops:
  0.1 0.9 copy-start.1
  25.5 21.6 %copy-start = (bf16[2,256,256]{2,1,0:T(8,128)(2,1)S(1)}, bf16[2,256,256]{2,1,0:T(8,128)(2,1)}, u32[]{:S(2)}) copy-start(bf16[2,256,256]{2,1,0:T(8,128)(2,1)} %diag_ref.1) | copy-start | bytes 786436
  25.5 21.6 %copy-start.3 = (s32[2,80]{1,0:T(2,128)S(1)}, s32[2,80]{1,0:T(2,128)}, u32[]{:S(2)}) copy-start(s32[2,80]{1,0:T(2,128)} %order_ref.1) | copy-start | bytes 1924
  50.8 9.7 %collective-permute-start.1 = (bf16[160,512]{1,0:T(8,128)(2,1)S(1)}, bf16[160,512]{1,0:T(8,128)(2,1)S(1)}, u32[]{:S(2)}, u32[]{:S(2)}) collective-permute-start(bf16[160,512]{1,0:T(8,128)(2,1)S(1)} %get-tuple-element.8), channel_id=1, source_target_pairs={{0,48},{16,0},{32,16},{48,32},{64,112},{80,64},{96,80},{112,96},{1... | collective-permute-start | bytes 491528 | tf_op jit(solution)/shard_map/ppermute | solution.py:112
  50.9 9.7 %collective-permute-start = (bf16[160,512]{1,0:T(8,128)(2,1)S(1)}, bf16[160,512]{1,0:T(8,128)(2,1)S(1)}, u32[]{:S(2)}, u32[]{:S(2)}) collective-permute-start(bf16[160,512]{1,0:T(8,128)(2,1)S(1)} %get-tuple-element.8), channel_id=1, source_target_pairs={{0,16},{16,32},{32,48},{48,0},{64,80},{80,96},{96,112},{112,64},{1... | collective-permute-start | bytes 491528 | tf_op jit(solution)/shard_map/ppermute | solution.py:111
  53.8 38.0 %copy-start.2 = (s32[80,80]{1,0:T(8,128)S(1)}, s32[80,80]{1,0:T(8,128)}, u32[]{:S(2)}) copy-start(s32[80,80]{1,0:T(8,128)} %mask_ref.1) | copy-start | bytes 76804
  60.5 6.9 %collective-permute-start.3 = (bf16[80,512]{1,0:T(8,128)(2,1)S(1)}, bf16[80,512]{1,0:T(8,128)(2,1)S(1)}, u32[]{:S(2)}, u32[]{:S(2)}) collective-permute-start(bf16[80,512]{1,0:T(8,128)(2,1)S(1)} %slice.17), channel_id=1, source_target_pairs={{0,48},{16,0},{32,16},{48,32},{64,112},{80,64},{96,80},{112,96},{1... | collective-permute-start | bytes 245768 | tf_op jit(solution)/shard_map/ppermute | solution.py:114
  60.6 6.8 %collective-permute-start.2 = (bf16[80,512]{1,0:T(8,128)(2,1)S(1)}, bf16[80,512]{1,0:T(8,128)(2,1)S(1)}, u32[]{:S(2)}, u32[]{:S(2)}) collective-permute-start(bf16[80,512]{1,0:T(8,128)(2,1)S(1)} %slice.16), channel_id=1, source_target_pairs={{0,16},{16,32},{32,48},{48,0},{64,80},{80,96},{96,112},{112,64},{1... | collective-permute-start | bytes 245768 | tf_op jit(solution)/shard_map/ppermute | solution.py:113
  67.4 13.6 %collective-permute-start.5 = (bf16[640,512]{1,0:T(8,128)(2,1)S(1)}, bf16[640,512]{1,0:T(8,128)(2,1)S(1)}, u32[]{:S(2)}, u32[]{:S(2)}) collective-permute-start(bf16[640,512]{1,0:T(8,128)(2,1)S(1)} %constant_dynamic-update-slice_fusion.o_ref), channel_id=1, source_target_pairs={{0,192},{16,208},{32,224},{48,240},{64,0},{80,16},{96,32},{112,48}... | collective-permute-start | bytes 1966088 | tf_op jit(solution)/shard_map/ppermute | solution.py:112
  68.5 14.9 %collective-permute-start.4 = (bf16[640,512]{1,0:T(8,128)(2,1)S(1)}, bf16[640,512]{1,0:T(8,128)(2,1)S(1)}, u32[]{:S(2)}, u32[]{:S(2)}) collective-permute-start(bf16[640,512]{1,0:T(8,128)(2,1)S(1)} %constant_dynamic-update-slice_fusion.o_ref), channel_id=1, source_target_pairs={{0,64},{16,80},{32,96},{48,112},{64,128},{80,144},{96,160},{112,17... | collective-permute-start | bytes 1966088 | tf_op jit(solution)/shard_map/ppermute | solution.py:111
  81.0 7.2 %collective-permute-start.7 = (bf16[320,512]{1,0:T(8,128)(2,1)S(1)}, bf16[320,512]{1,0:T(8,128)(2,1)S(1)}, u32[]{:S(2)}, u32[]{:S(2)}) collective-permute-start(bf16[320,512]{1,0:T(8,128)(2,1)S(1)} %slice.19), channel_id=1, source_target_pairs={{0,192},{16,208},{32,224},{48,240},{64,0},{80,16},{96,32},{112,48}... | collective-permute-start | bytes 983048 | tf_op jit(solution)/shard_map/ppermute | solution.py:114
  83.4 8.4 %collective-permute-start.6 = (bf16[320,512]{1,0:T(8,128)(2,1)S(1)}, bf16[320,512]{1,0:T(8,128)(2,1)S(1)}, u32[]{:S(2)}, u32[]{:S(2)}) collective-permute-start(bf16[320,512]{1,0:T(8,128)(2,1)S(1)} %slice.18), channel_id=1, source_target_pairs={{0,64},{16,80},{32,96},{48,112},{64,128},{80,144},{96,160},{112,17... | collective-permute-start | bytes 983048 | tf_op jit(solution)/shard_map/ppermute | solution.py:113

commit v2 on v0

v2 whole, which is shorter than its diff:
```python
import jax
import jax.numpy as jnp
from jax import lax
from jax.experimental import pallas as pl
from jax.experimental.pallas import tpu as pltpu
from jax.sharding import Mesh
from jax.sharding import PartitionSpec as P

NX, NZ, NL, NY = 4, 4, 2, 4
SLICE = 16
LANES = 128
VMEM = pltpu.VMEM
SMEM = pltpu.SMEM


def whole(space=VMEM):
    return pl.BlockSpec(memory_space=space)


def params():
    return pltpu.CompilerParams(vmem_limit_bytes=48 * 1024 * 1024)


def spread_kernel(pos_ref, l_ref, out_ref):
    snodes, rows, _ = l_ref.shape
    count = rows // SLICE
    first = (pos_ref[2] * NY + pos_ref[3]) * count
    for i in range(count):
        k = (first + i) & (NX * NY - 1)
        for l in range(NL):
            slot = ((k // NY) * NL + l) * NY + (k & (NY - 1))
            for s in range(snodes):
                out_ref[slot, s] = l_ref[s, i * SLICE : (i + 1) * SLICE, l * LANES : (l + 1) * LANES]


def compact_kernel(pos_ref, got_ref, out_ref):
    snodes = got_ref.shape[1]
    per_row = out_ref.shape[0] // (NX * snodes)
    count = per_row * NX * NY // (NL * NY)
    k = pos_ref[0] * NY + pos_ref[3]
    for t in range(per_row):
        col = (t * NX * NY + k) // count
        for x in range(NX):
            for s in range(snodes):
                out_ref[(x * per_row + t) * snodes + s] = got_ref[x * NL * NY + col, s]


def route_kernel(pos_ref, order_ref, all_ref, out_ref):
    snodes, blocks = order_ref.shape
    per_row = blocks // (NX * NZ)
    part = NX * per_row * snodes
    for z in range(NZ):
        d = (z - pos_ref[1]) & (NZ - 1)
        base = jnp.where(d == 0, 0, jnp.where(d == 3, 1, jnp.where(d == 1, 2, 3))) * part
        for x in range(NX):
            for t in range(per_row):
                q = (x * NZ + z) * per_row + t
                for s in range(snodes):
                    out_ref[order_ref[s, q], s] = all_ref[base + (x * per_row + t) * snodes + s]


def normal_kernel(got_ref, diag_ref, out_ref, picked):
    _, share, snodes = got_ref.shape[:3]
    tile = diag_ref.shape[1]
    for s in range(snodes):
        for a in range(share):
            for y in range(NY):
                at = (a * NY + y) * SLICE
                for l in range(NL):
                    picked[at : at + SLICE, l * LANES : (l + 1) * LANES] = got_ref[l * NY + y, a, s]
        out_ref[:, s * tile : (s + 1) * tile] = jnp.dot(
            picked[...], diag_ref[s], preferred_element_type=jnp.float32
        ).astype(out_ref.dtype)


def product_kernel(pos_ref, mask_ref, a_ref, o_ref, u_ref, d_ref, fu_ref, fd_ref, out_ref, stacked):
    i = pl.program_id(0)
    quarter = NY * SLICE
    tile = NX * quarter
    share = stacked.shape[0] // tile

    @pl.when(i == 0)
    def _():
        for a in range(share):
            far, at = (fu_ref, a) if a < share // 2 else (fd_ref, a - share // 2)
            for shift, ref, n in ((0, o_ref, a), (-1, u_ref, a), (1, d_ref, a), (2, far, at)):
                x = (pos_ref[0] + shift) & (NX - 1)
                stacked[pl.ds(pl.multiple_of(a * tile + x * quarter, quarter), quarter), :] = ref[
                    n * quarter : (n + 1) * quarter, :
                ]

    gates = []
    row = (pos_ref[0] * NZ + pos_ref[1]) * pl.num_programs(0) + i
    col = (pos_ref[2] * NY + pos_ref[3]) * share
    for j in range(share):
        keep = jnp.full((1, tile), mask_ref[row, col + j], jnp.int32).astype(jnp.float32)
        gates.append(keep.astype(jnp.bfloat16))
    gate_row = jnp.concatenate(gates, axis=1)
    out_ref[...] = (
        -jnp.dot(a_ref[...] * gate_row, stacked[...], preferred_element_type=jnp.float32)
    ).astype(out_ref.dtype)


def ring(value, axis):
    size = lax.axis_size(axis)
    up = [(i, (i + 1) % size) for i in range(size)]
    down = [(i, (i - 1) % size) for i in range(size)]
    half = value.shape[0] // 2
    from_up = lax.ppermute(value, axis, up)
    from_down = lax.ppermute(value, axis, down)
    far_up = lax.ppermute(from_up[:half], axis, up)
    far_down = lax.ppermute(from_down[half:], axis, down)
    return value, from_up, from_down, far_up, far_down


def per_device(ancestor_inverse, fill_mask, block_order, l_rows, diag_inverse):
    snodes, tile = diag_inverse.shape[0], diag_inverse.shape[1]
    local_rows, local_cols = ancestor_inverse.shape
    blocks = block_order.shape[1]
    cols = NL * NY
    share = blocks // cols
    width = snodes * tile
    bf16 = jnp.bfloat16
    pos = jnp.stack([lax.axis_index(name) for name in ("x", "z", "l", "y")]).astype(jnp.int32)

    spread = pl.pallas_call(
        spread_kernel,
        out_shape=jax.ShapeDtypeStruct((NX * cols, snodes, SLICE, LANES), bf16),
        in_specs=[whole(SMEM), whole()],
        out_specs=whole(),
        compiler_params=params(),
        name="spread",
    )(pos, l_rows)
    got = lax.all_to_all(spread, ("x", "l", "y"), 0, 0, tiled=True)
    mine = pl.pallas_call(
        compact_kernel,
        out_shape=jax.ShapeDtypeStruct((blocks // NZ * snodes, SLICE, LANES), bf16),
        in_specs=[whole(SMEM), whole()],
        out_specs=whole(),
        compiler_params=params(),
        name="compact",
    )(pos, got)
    everything = jnp.concatenate(ring(mine, "z"), axis=0)
    routed = pl.pallas_call(
        route_kernel,
        out_shape=jax.ShapeDtypeStruct((blocks, snodes, SLICE, LANES), bf16),
        in_specs=[whole(SMEM), whole(SMEM), whole()],
        out_specs=whole(),
        compiler_params=params(),
        name="route",
    )(pos, block_order, everything)
    quarters = lax.all_to_all(routed, ("l", "y"), 0, 0, tiled=True)
    own = pl.pallas_call(
        normal_kernel,
        out_shape=jax.ShapeDtypeStruct((share * NY * SLICE, width), bf16),
        in_specs=[whole(), whole()],
        out_specs=whole(),
        scratch_shapes=[VMEM((share * NY * SLICE, tile), bf16)],
        compiler_params=params(),
        name="normal",
    )(quarters.reshape(cols, share, snodes, SLICE, LANES), diag_inverse)
    partial_value = pl.pallas_call(
        product_kernel,
        out_shape=jax.ShapeDtypeStruct((local_rows, width), bf16),
        grid=(local_rows // tile,),
        in_specs=[whole(SMEM), whole(SMEM), pl.BlockSpec((tile, local_cols), lambda i: (i, 0))] + [whole()] * 5,
        out_specs=pl.BlockSpec((tile, width), lambda i: (i, 0)),
        scratch_shapes=[VMEM((local_cols, width), bf16)],
        compiler_params=params(),
        name="product",
    )(pos, fill_mask, ancestor_inverse, *ring(own, "x"))
    share_rows = local_rows // cols
    shares = lax.all_to_all(partial_value, ("l", "y"), 0, 0, tiled=True)
    summed = shares.reshape(cols, share_rows, snodes, tile).astype(jnp.float32).sum(0)
    return summed.transpose(1, 2, 0).astype(bf16)


def solution(mesh):
    fine = Mesh(
        mesh.devices.reshape(NX, NZ, NL, NY, mesh.shape["snode"]), ("x", "z", "l", "y", "snode")
    )
    row, col = ("x", "z"), ("l", "y")
    return jax.shard_map(
        per_device,
        mesh=fine,
        in_specs=(
            P(("snode", *row), col),
            P("snode", None),
            P("snode", None),
            P("snode", (*row, *col), None),
            P("snode", None, None),
        ),
        out_specs=P("snode", None, (*row, *col)),
        check_vma=False,
    )
```

time: 299 us -> 102 us (0.34)
  waiting for transfers between devices: 232 us -> 32.1 us
  blocking collectives: 0 us -> 43.8 us
  matrix products: 29.9 us -> 0 us
  local copies, waits for them, and re-layouts: 20.7 us -> 1.81 us
  starting transfers between devices: 0.04 us -> 14.4 us
  between operations: 13.5 us -> 0.13 us
  Pallas kernels: 0 us -> 9.02 us
    all_gather x1 -> x0, waiting for transfers between devices: 151 us -> none  [per_device(): everything = lax.all_gather(normed, ('row', 'col'), axis=1, tiled=True)]
    psum x1 -> x0, waiting for transfers between devices: 81.4 us -> none  [per_device(): lax.psum(partial_value.astype(jnp.bfloat16), 'col').astype(jnp.float32)]
    all_to_all x0 -> x3, blocking collectives: none -> 43.8 us  [the longest x1 16.4 us: per_device(): got = lax.all_to_all(spread, ('x', 'l', 'y'), 0, 0, tiled=True)]
    ppermute x0 -> x8, waiting for transfers between devices: none -> 32.1 us  [the longest x2 17.7 us: ring(): from_down = lax.ppermute(value, axis, down)]
    dot_general x3 -> x0, matrix products: 29.9 us -> none  [the longest x1 20.5 us: per_device(): jnp.einsum('saq,sqxy->saxy', selector, pieces, preferred_element_type=jnp...]
    ppermute x0 -> x8, starting transfers between devices: none -> 14.4 us  [the longest x2 6.79 us: ring(): from_down = lax.ppermute(value, axis, down)]
    unnamed x8 -> x12, local copies, waits for them, and re-layouts: 12.6 us -> 1.01 us
    pallas_call x0 -> x5, Pallas kernels: none -> 9.02 us  [the longest x1 6.76 us: per_device(): pl.pallas_call(product_kernel, out_shape=jax.ShapeDtypeStruct((local_rows...]
  transfers between devices with their start and end apart: 2 -> 8, of which waited for: 2 -> 6; matrix products, arithmetic and copies ran while one was open for 6% -> 0% of each run, Pallas kernels for 0% -> 0%
where the time goes in v2:
time: 102 us
  blocking collectives  43.8 us (43%)
  waiting for transfers between devices  32.1 us (31%)
  starting transfers between devices  14.4 us (14%)
  Pallas kernels  9.02 us (9%)
  local copies, waits for them, and re-layouts  1.81 us (2%)
    ppermute x2, waiting for transfers between devices, ring(): from_down = lax.ppermute(value, axis, down)  17.7 us
    all_to_all x1, blocking collectives, per_device(): got = lax.all_to_all(spread, ('x', 'l', 'y'), 0, 0, tiled=True)  16.4 us
    all_to_all x1, blocking collectives, per_device(): shares = lax.all_to_all(partial_value, ('l', 'y'), 0, 0, tiled=True)  15.3 us
    all_to_all x1, blocking collectives, per_device(): quarters = lax.all_to_all(routed, ('l', 'y'), 0, 0, tiled=True)  12.1 us
    ppermute x2, waiting for transfers between devices, ring(): far_up = lax.ppermute(from_up[:half], axis, up)  9.03 us
    ppermute x2, starting transfers between devices, ring(): from_down = lax.ppermute(value, axis, down)  6.79 us
    pallas_call x1, Pallas kernels, per_device(): pl.pallas_call(product_kernel, out_shape=jax.ShapeDtypeStruct((local_rows...  6.76 us
    ppermute x2, starting transfers between devices, ring(): far_down = lax.ppermute(from_down[half:], axis, down)  5.96 us
  transfers between devices with their start and end apart: 8, of which 6 were waited for; matrix products, arithmetic and copies ran while one was open for 0% of the time, Pallas kernels for 0%

profile of v2, /device:TPU:32, one launch (start us, length us, event | category | flops | bytes accessed | tf_op | source)
XLA Modules:
  0.0 101.6 jit_solution(13568992289821701164)
XLA Ops:
  0.0 0.1 pad_add_fusion.pos_ref
  0.1 0.0 copy-start.1
  0.1 0.9 copy-done.1
  1.0 0.6 spread.1
  1.6 0.0 copy-start.3
  1.6 16.4 %all_to_all.19.got_ref = bf16[32,2,16,128]{3,2,1,0:T(8,128)(2,1)S(1)} all-to-all(bf16[32,2,16,128]{3,2,1,0:T(8,128)(2,1)S(1)} %spread.1), channel_id=1, replica_groups=mesh['x'=4,'z'=4,'l'=2,'y'=4,'snode'=2] {'x','l','y'}, dimensions={0} | all-to-all | bytes 524288 | tf_op jit(solution)/shard_map/all_to_all | solution.py:134
  18.0 0.6 compact.1
  18.6 5.5 %collective-permute-start.1 = (bf16[40,16,128]{2,1,0:T(8,128)(2,1)S(1)}, bf16[40,16,128]{2,1,0:T(8,128)(2,1)S(1)}, u32[]{:S(2)}, u32[]{:S(2)}) collective-permute-start(bf16[40,16,128]{2,1,0:T(8,128)(2,1)S(1)} %compact.1), channel_id=1, source_target_pairs={{0,48},{16,0},{32,16},{48,32},{1,49},{17,1},{33,17},{49,33},{2,50}... | collective-permute-start | bytes 491528 | tf_op jit(solution)/shard_map/ppermute | solution.py:110
  24.1 0.0 collective-permute-start
  24.1 4.9 %collective-permute-done.1 = bf16[40,16,128]{2,1,0:T(8,128)(2,1)S(1)} collective-permute-done((bf16[40,16,128]{2,1,0:T(8,128)(2,1)S(1)}, bf16[40,16,128]{2,1,0:T(8,128)(2,1)S(1)}, u32[]{:S(2)}, u32[]{:S(2)}) %collective-permute-start.1) | collective-permute-done | bytes 163872 | tf_op jit(solution)/shard_map/ppermute | solution.py:110
  29.1 4.6 %collective-permute-start.3 = (bf16[20,16,128]{2,1,0:T(8,128)(2,1)S(1)}, bf16[20,16,128]{2,1,0:T(8,128)(2,1)S(1)}, u32[]{:S(2)}, u32[]{:S(2)}) collective-permute-start(bf16[20,16,128]{2,1,0:T(8,128)(2,1)S(1)} %slice.17), channel_id=1, source_target_pairs={{0,48},{16,0},{32,16},{48,32},{1,49},{17,1},{33,17},{49,33},{2,50}... | collective-permute-start | bytes 245768 | tf_op jit(solution)/shard_map/ppermute | solution.py:112
  33.7 0.4 collective-permute-done
  34.2 0.0 collective-permute-start.2
  34.2 6.5 %collective-permute-done.2 = bf16[20,16,128]{2,1,0:T(8,128)(2,1)S(1)} collective-permute-done((bf16[20,16,128]{2,1,0:T(8,128)(2,1)S(1)}, bf16[20,16,128]{2,1,0:T(8,128)(2,1)S(1)}, u32[]{:S(2)}, u32[]{:S(2)}) %collective-permute-start.2) | collective-permute-done | bytes 81952 | tf_op jit(solution)/shard_map/ppermute | solution.py:111
  40.7 0.0 collective-permute-done.3
  40.8 0.0 copy-done.3
  40.8 0.0 copy-start
  40.8 0.7 route.1
  41.5 12.1 %all_to_all.20 = bf16[80,2,16,128]{3,2,1,0:T(8,128)(2,1)S(1)} all-to-all(bf16[80,2,16,128]{3,2,1,0:T(8,128)(2,1)S(1)} %route.1), channel_id=1, replica_groups=mesh['x'=4,'z'=4,'l'=2,'y'=4,'snode'=2] {'l','y'}, dimensions={0} | all-to-all | bytes 1310720 | tf_op jit(solution)/shard_map/all_to_all | solution.py:152
  53.6 0.0 copy-done
  53.6 0.0 copy-start.2
  53.6 0.4 normal.1.o_ref
  54.0 1.3 %collective-permute-start.5 = (bf16[640,512]{1,0:T(8,128)(2,1)S(1)}, bf16[640,512]{1,0:T(8,128)(2,1)S(1)}, u32[]{:S(2)}, u32[]{:S(2)}) collective-permute-start(bf16[640,512]{1,0:T(8,128)(2,1)S(1)} %normal.1.o_ref), channel_id=1, source_target_pairs={{0,192},{64,0},{128,64},{192,128},{1,193},{65,1},{129,65},{193,129... | collective-permute-start | bytes 1966088 | tf_op jit(solution)/shard_map/ppermute | solution.py:110
  55.3 0.8 collective-permute-start.4
  56.1 12.8 %collective-permute-done.5.d_ref = bf16[640,512]{1,0:T(8,128)(2,1)S(1)} collective-permute-done((bf16[640,512]{1,0:T(8,128)(2,1)S(1)}, bf16[640,512]{1,0:T(8,128)(2,1)S(1)}, u32[]{:S(2)}, u32[]{:S(2)}) %collective-permute-start.5) | collective-permute-done | bytes 655392 | tf_op jit(solution)/shard_map/ppermute | solution.py:110
  68.9 1.3 %collective-permute-start.7 = (bf16[320,512]{1,0:T(8,128)(2,1)S(1)}, bf16[320,512]{1,0:T(8,128)(2,1)S(1)}, u32[]{:S(2)}, u32[]{:S(2)}) collective-permute-start(bf16[320,512]{1,0:T(8,128)(2,1)S(1)} %slice.19), channel_id=1, source_target_pairs={{0,192},{64,0},{128,64},{192,128},{1,193},{65,1},{129,65},{193,129... | collective-permute-start | bytes 983048 | tf_op jit(solution)/shard_map/ppermute | solution.py:112
  70.2 0.0 collective-permute-done.4.u_ref
  70.2 0.9 collective-permute-start.6
  71.1 4.9 %collective-permute-done.7.fd_ref = bf16[320,512]{1,0:T(8,128)(2,1)S(1)} collective-permute-done((bf16[320,512]{1,0:T(8,128)(2,1)S(1)}, bf16[320,512]{1,0:T(8,128)(2,1)S(1)}, u32[]{:S(2)}, u32[]{:S(2)}) %collective-permute-start.7) | collective-permute-done | bytes 327712 | tf_op jit(solution)/shard_map/ppermute | solution.py:112
  76.0 2.6 %collective-permute-done.6.fu_ref = bf16[320,512]{1,0:T(8,128)(2,1)S(1)} collective-permute-done((bf16[320,512]{1,0:T(8,128)(2,1)S(1)}, bf16[320,512]{1,0:T(8,128)(2,1)S(1)}, u32[]{:S(2)}, u32[]{:S(2)}) %collective-permute-start.6) | collective-permute-done | bytes 327712 | tf_op jit(solution)/shard_map/ppermute | solution.py:111
  78.6 0.0 copy-done.2
  78.6 6.8 %product.1 = bf16[1280,512]{1,0:T(8,128)(2,1)S(1)} custom-call(s32[4]{0:T(128)S(1)} %pad_add_fusion.pos_ref, s32[80,80]{1,0:T(8,128)S(1)} %copy-done.2, bf16[1280,2560]{1,0:T(8,128)(2,1)} %a_ref.1, bf16[640,512]{1,0:T(8,128)(2,1)S(1)} %normal.1.o_ref, bf16[640,512]{1,0:T(8,128)(2,1)S(1)} %collective-permute-done.4.u_ref, ...), custom_call_target="tpu_custom_call" | custom-call | tf_op jit(solution)/shard_map/product/pallas_call | solution.py:162
  85.4 15.3 %all_to_all.21 = bf16[8,160,512]{2,1,0:T(8,128)(2,1)S(1)} all-to-all(bf16[8,160,512]{2,1,0:T(8,128)(2,1)S(1)} %bitcast.7), channel_id=1, replica_groups=mesh['x'=4,'z'=4,'l'=2,'y'=4,'snode'=2] {'l','y'}, dimensions={0} | all-to-all | bytes 2621440 | tf_op jit(solution)/shard_map/all_to_all | solution.py:173
  100.7 0.2 reduce_sum.12
  100.9 0.7 copy.6
  (10 shorter events, 0.2 us)
Async XLA Ops:
  0.1 0.9 copy-start.1
  1.6 39.2 %copy-start.3 = (s32[2,80]{1,0:T(2,128)S(1)}, s32[2,80]{1,0:T(2,128)}, u32[]{:S(2)}) copy-start(s32[2,80]{1,0:T(2,128)} %order_ref.1) | copy-start | bytes 1924
  18.6 10.4 %collective-permute-start.1 = (bf16[40,16,128]{2,1,0:T(8,128)(2,1)S(1)}, bf16[40,16,128]{2,1,0:T(8,128)(2,1)S(1)}, u32[]{:S(2)}, u32[]{:S(2)}) collective-permute-start(bf16[40,16,128]{2,1,0:T(8,128)(2,1)S(1)} %compact.1), channel_id=1, source_target_pairs={{0,48},{16,0},{32,16},{48,32},{1,49},{17,1},{33,17},{49,33},{2,50}... | collective-permute-start | bytes 491528 | tf_op jit(solution)/shard_map/ppermute | solution.py:110
  24.1 10.1 %collective-permute-start = (bf16[40,16,128]{2,1,0:T(8,128)(2,1)S(1)}, bf16[40,16,128]{2,1,0:T(8,128)(2,1)S(1)}, u32[]{:S(2)}, u32[]{:S(2)}) collective-permute-start(bf16[40,16,128]{2,1,0:T(8,128)(2,1)S(1)} %compact.1), channel_id=1, source_target_pairs={{0,16},{16,32},{32,48},{48,0},{1,17},{17,33},{33,49},{49,1},{2,18}... | collective-permute-start | bytes 491528 | tf_op jit(solution)/shard_map/ppermute | solution.py:109
  29.1 11.7 %collective-permute-start.3 = (bf16[20,16,128]{2,1,0:T(8,128)(2,1)S(1)}, bf16[20,16,128]{2,1,0:T(8,128)(2,1)S(1)}, u32[]{:S(2)}, u32[]{:S(2)}) collective-permute-start(bf16[20,16,128]{2,1,0:T(8,128)(2,1)S(1)} %slice.17), channel_id=1, source_target_pairs={{0,48},{16,0},{32,16},{48,32},{1,49},{17,1},{33,17},{49,33},{2,50}... | collective-permute-start | bytes 245768 | tf_op jit(solution)/shard_map/ppermute | solution.py:112
  34.2 6.6 %collective-permute-start.2 = (bf16[20,16,128]{2,1,0:T(8,128)(2,1)S(1)}, bf16[20,16,128]{2,1,0:T(8,128)(2,1)S(1)}, u32[]{:S(2)}, u32[]{:S(2)}) collective-permute-start(bf16[20,16,128]{2,1,0:T(8,128)(2,1)S(1)} %slice.16), channel_id=1, source_target_pairs={{0,16},{16,32},{32,48},{48,0},{1,17},{17,33},{33,49},{49,1},{2,18}... | collective-permute-start | bytes 245768 | tf_op jit(solution)/shard_map/ppermute | solution.py:111
  40.8 12.8 %copy-start = (bf16[2,256,256]{2,1,0:T(8,128)(2,1)S(1)}, bf16[2,256,256]{2,1,0:T(8,128)(2,1)}, u32[]{:S(2)}) copy-start(bf16[2,256,256]{2,1,0:T(8,128)(2,1)} %diag_ref.1) | copy-start | bytes 786436
  53.6 25.0 %copy-start.2 = (s32[80,80]{1,0:T(8,128)S(1)}, s32[80,80]{1,0:T(8,128)}, u32[]{:S(2)}) copy-start(s32[80,80]{1,0:T(8,128)} %mask_ref.1) | copy-start | bytes 76804
  54.0 14.9 %collective-permute-start.5 = (bf16[640,512]{1,0:T(8,128)(2,1)S(1)}, bf16[640,512]{1,0:T(8,128)(2,1)S(1)}, u32[]{:S(2)}, u32[]{:S(2)}) collective-permute-start(bf16[640,512]{1,0:T(8,128)(2,1)S(1)} %normal.1.o_ref), channel_id=1, source_target_pairs={{0,192},{64,0},{128,64},{192,128},{1,193},{65,1},{129,65},{193,129... | collective-permute-start | bytes 1966088 | tf_op jit(solution)/shard_map/ppermute | solution.py:110
  55.3 14.9 %collective-permute-start.4 = (bf16[640,512]{1,0:T(8,128)(2,1)S(1)}, bf16[640,512]{1,0:T(8,128)(2,1)S(1)}, u32[]{:S(2)}, u32[]{:S(2)}) collective-permute-start(bf16[640,512]{1,0:T(8,128)(2,1)S(1)} %normal.1.o_ref), channel_id=1, source_target_pairs={{0,64},{64,128},{128,192},{192,0},{1,65},{65,129},{129,193},{193,1... | collective-permute-start | bytes 1966088 | tf_op jit(solution)/shard_map/ppermute | solution.py:109
  68.9 7.2 %collective-permute-start.7 = (bf16[320,512]{1,0:T(8,128)(2,1)S(1)}, bf16[320,512]{1,0:T(8,128)(2,1)S(1)}, u32[]{:S(2)}, u32[]{:S(2)}) collective-permute-start(bf16[320,512]{1,0:T(8,128)(2,1)S(1)} %slice.19), channel_id=1, source_target_pairs={{0,192},{64,0},{128,64},{192,128},{1,193},{65,1},{129,65},{193,129... | collective-permute-start | bytes 983048 | tf_op jit(solution)/shard_map/ppermute | solution.py:112
  70.2 8.4 %collective-permute-start.6 = (bf16[320,512]{1,0:T(8,128)(2,1)S(1)}, bf16[320,512]{1,0:T(8,128)(2,1)S(1)}, u32[]{:S(2)}, u32[]{:S(2)}) collective-permute-start(bf16[320,512]{1,0:T(8,128)(2,1)S(1)} %slice.18), channel_id=1, source_target_pairs={{0,64},{64,128},{128,192},{192,0},{1,65},{65,129},{129,193},{193,1... | collective-permute-start | bytes 983048 | tf_op jit(solution)/shard_map/ppermute | solution.py:111

commit v3 on v2

--- a/solution.py
+++ b/solution.py
@@ -1,3 +1,5 @@
+import functools
+
 import jax
 import jax.numpy as jnp
 from jax import lax
@@ -18,7 +20,11 @@
 
 
 def params():
-    return pltpu.CompilerParams(vmem_limit_bytes=48 * 1024 * 1024)
+    return pltpu.CompilerParams(vmem_limit_bytes=24 * 1024 * 1024)
+
+
+def place_of(x):
+    return ((x & 1) * 2 + x // 2) * NY
 
 
 def spread_kernel(pos_ref, l_ref, out_ref):
@@ -28,7 +34,8 @@
     for i in range(count):
         k = (first + i) & (NX * NY - 1)
         for l in range(NL):
-            slot = ((k // NY) * NL + l) * NY + (k & (NY - 1))
+            x = ((k // NY) & 1) * 2 + k // (2 * NY)
+            slot = (x * NL + l) * NY + (k & (NY - 1))
             for s in range(snodes):
                 out_ref[slot, s] = l_ref[s, i * SLICE : (i + 1) * SLICE, l * LANES : (l + 1) * LANES]
 
@@ -37,7 +44,7 @@
     snodes = got_ref.shape[1]
     per_row = out_ref.shape[0] // (NX * snodes)
     count = per_row * NX * NY // (NL * NY)
-    k = pos_ref[0] * NY + pos_ref[3]
+    k = place_of(pos_ref[0]) + pos_ref[3]
     for t in range(per_row):
         col = (t * NX * NY + k) // count
         for x in range(NX):
@@ -73,32 +80,59 @@
         ).astype(out_ref.dtype)
 
 
-def product_kernel(pos_ref, mask_ref, a_ref, o_ref, u_ref, d_ref, fu_ref, fd_ref, out_ref, stacked):
-    i = pl.program_id(0)
+def fill(stacked, pairs):
     quarter = NY * SLICE
-    tile = NX * quarter
-    share = stacked.shape[0] // tile
-
-    @pl.when(i == 0)
-    def _():
+    share = stacked.shape[0] // (2 * quarter)
+    for x, refs in pairs:
+        each = share // len(refs)
         for a in range(share):
-            far, at = (fu_ref, a) if a < share // 2 else (fd_ref, a - share // 2)
-            for shift, ref, n in ((0, o_ref, a), (-1, u_ref, a), (1, d_ref, a), (2, far, at)):
-                x = (pos_ref[0] + shift) & (NX - 1)
-                stacked[pl.ds(pl.multiple_of(a * tile + x * quarter, quarter), quarter), :] = ref[
-                    n * quarter : (n + 1) * quarter, :
-                ]
-
-    gates = []
-    row = (pos_ref[0] * NZ + pos_ref[1]) * pl.num_programs(0) + i
+            at = pl.multiple_of(a * 2 * quarter + (x // 2) * quarter, quarter)
+            n = a % each
+            stacked[pl.ds(at, quarter), :] = refs[a // each][n * quarter : (n + 1) * quarter, :]
+
+
+def gate_kernel(own_half, pos_ref, mask_ref, a_ref, _after, out_ref, arrived):
+    rows, half = out_ref.shape
+    share = half // LANES
+    tile = 2 * LANES
+    x = pos_ref[0]
+    side = (x & 1) if own_half else 1 - (x & 1)
+    copies = []
+    for a in range(share):
+        columns = pl.ds(pl.multiple_of(a * tile + side * LANES, LANES), LANES)
+        copies.append(
+            pltpu.make_async_copy(a_ref.at[:, columns], out_ref.at[:, a * LANES : (a + 1) * LANES], arrived.at[a])
+        )
+        copies[a].start()
+    row = (x * NZ + pos_ref[1]) * (rows // tile)
     col = (pos_ref[2] * NY + pos_ref[3]) * share
-    for j in range(share):
-        keep = jnp.full((1, tile), mask_ref[row, col + j], jnp.int32).astype(jnp.float32)
-        gates.append(keep.astype(jnp.bfloat16))
-    gate_row = jnp.concatenate(gates, axis=1)
-    out_ref[...] = (
-        -jnp.dot(a_ref[...] * gate_row, stacked[...], preferred_element_type=jnp.float32)
-    ).astype(out_ref.dtype)
+    for a in range(share):
+        copies[a].wait()
+        at = slice(a * LANES, (a + 1) * LANES)
+        for i in range(rows // tile):
+            keep = jnp.full((1, LANES), mask_ref[row + i, col + a], jnp.int32).astype(jnp.float32)
+            down = slice(i * tile, (i + 1) * tile)
+            out_ref[down, at] = out_ref[down, at] * keep.astype(jnp.bfloat16)
+
+
+def near_kernel(pos_ref, a_ref, ul_ref, uh_ref, dl_ref, dh_ref, out_ref, stacked):
+    x = pos_ref[0]
+    fill(stacked, (((x - 1) & (NX - 1), (ul_ref, uh_ref)), ((x + 1) & (NX - 1), (dl_ref, dh_ref))))
+    tile = 2 * LANES
+    for n in range(out_ref.shape[1] // tile):
+        at = slice(n * tile, (n + 1) * tile)
+        out_ref[:, at] = jnp.dot(a_ref[...], stacked[:, at], preferred_element_type=jnp.float32)
+
+
+def far_kernel(pos_ref, a_ref, near_ref, own_ref, fu_ref, fd_ref, out_ref, stacked):
+    x = pos_ref[0]
+    fill(stacked, ((x, (own_ref,)), ((x + 2) & (NX - 1), (fu_ref, fd_ref))))
+    tile = 2 * LANES
+    for n in range(out_ref.shape[1] // tile):
+        at = slice(n * tile, (n + 1) * tile)
+        out_ref[:, at] = (
+            -(near_ref[:, at] + jnp.dot(a_ref[...], stacked[:, at], preferred_element_type=jnp.float32))
+        ).astype(out_ref.dtype)
 
 
 def ring(value, axis):
@@ -113,6 +147,22 @@
     return value, from_up, from_down, far_up, far_down
 
 
+def split_ring(value, axis, beside):
+    size = lax.axis_size(axis)
+    up = [(i, (i + 1) % size) for i in range(size)]
+    down = [(i, (i - 1) % size) for i in range(size)]
+    half = value.shape[0] // 2
+    low, high = value[:half], value[half:]
+    up_low = lax.ppermute(low, axis, up)
+    down_high = lax.ppermute(high, axis, down)
+    up_high = lax.ppermute(high, axis, up)
+    down_low = lax.ppermute(low, axis, down)
+    up_low, down_high, made = lax.optimization_barrier((up_low, down_high, beside()))
+    far_up = lax.ppermute(up_low, axis, up)
+    far_down = lax.ppermute(down_high, axis, down)
+    return (value, up_low, up_high, down_low, down_high, far_up, far_down), made
+
+
 def per_device(ancestor_inverse, fill_mask, block_order, l_rows, diag_inverse):
     snodes, tile = diag_inverse.shape[0], diag_inverse.shape[1]
     local_rows, local_cols = ancestor_inverse.shape
@@ -140,6 +190,22 @@
         compiler_params=params(),
         name="compact",
     )(pos, got)
+    half_cols = local_cols // 2
+
+    def gate(own_half, after):
+        return pl.pallas_call(
+            functools.partial(gate_kernel, own_half),
+            out_shape=jax.ShapeDtypeStruct((local_rows, half_cols), bf16),
+            in_specs=[whole(SMEM), whole(SMEM), whole(pl.ANY), whole(pl.ANY)],
+            out_specs=whole(),
+            scratch_shapes=[pltpu.SemaphoreType.DMA((share,))],
+            compiler_params=params(),
+            cost_estimate=pl.CostEstimate(
+                flops=local_rows * half_cols, bytes_accessed=4 * local_rows * half_cols, transcendentals=0
+            ),
+            name="gate",
+        )(pos, fill_mask, ancestor_inverse, after)
+
     everything = jnp.concatenate(ring(mine, "z"), axis=0)
     routed = pl.pallas_call(
         route_kernel,
@@ -159,16 +225,29 @@
         compiler_params=params(),
         name="normal",
     )(quarters.reshape(cols, share, snodes, SLICE, LANES), diag_inverse)
+    (own, *near, far_up, far_down), gated_own = split_ring(own, "x", lambda: gate(True, own))
+    gated_other = gate(False, own)
+    near_value = pl.pallas_call(
+        near_kernel,
+        out_shape=jax.ShapeDtypeStruct((local_rows, width), jnp.float32),
+        in_specs=[whole(SMEM)] + [whole()] * 5,
+        out_specs=whole(),
+        scratch_shapes=[VMEM((half_cols, width), bf16)],
+        compiler_params=params(),
+        cost_estimate=pl.CostEstimate(
+            flops=local_rows * local_cols * width, bytes_accessed=0, transcendentals=0
+        ),
+        name="near",
+    )(pos, gated_other, *near)
     partial_value = pl.pallas_call(
-        product_kernel,
+        far_kernel,
         out_shape=jax.ShapeDtypeStruct((local_rows, width), bf16),
-        grid=(local_rows // tile,),
-        in_specs=[whole(SMEM), whole(SMEM), pl.BlockSpec((tile, local_cols), lambda i: (i, 0))] + [whole()] * 5,
-        out_specs=pl.BlockSpec((tile, width), lambda i: (i, 0)),
-        scratch_shapes=[VMEM((local_cols, width), bf16)],
-        compiler_params=params(),
-        name="product",
-    )(pos, fill_mask, ancestor_inverse, *ring(own, "x"))
+        in_specs=[whole(SMEM)] + [whole()] * 5,
+        out_specs=whole(),
+        scratch_shapes=[VMEM((half_cols, width), bf16)],
+        compiler_params=params(),
+        name="far",
+    )(pos, gated_own, near_value, own, far_up, far_down)
     share_rows = local_rows // cols
     shares = lax.all_to_all(partial_value, ("l", "y"), 0, 0, tiled=True)
     summed = shares.reshape(cols, share_rows, snodes, tile).astype(jnp.float32).sum(0)

time: 102 us -> 95.2 us (0.933)
  waiting for transfers between devices: 32.1 us -> 13.1 us
  starting transfers between devices: 14.4 us -> 19.6 us
  Pallas kernels: 9.02 us -> 12.4 us
  blocking collectives: 43.8 us -> 46.4 us
    ppermute x2 -> x1, waiting for transfers between devices: 17.7 us -> 0.01 us  [ring(): from_down = lax.ppermute(value, axis, down)]
    ppermute x0 -> x6, starting transfers between devices: none -> 9.78 us  [the longest x1 3.24 us: split_ring(): far_down = lax.ppermute(down_high, axis, down)]
    ppermute x2 -> x1, waiting for transfers between devices: 9.03 us -> 2.26 us  [ring(): far_up = lax.ppermute(from_up[:half], axis, up)]
    ppermute x2 -> x1, waiting for transfers between devices: 0.44 us -> 5.36 us  [ring(): from_up = lax.ppermute(value, axis, up)]
    ppermute x2 -> x1, starting transfers between devices: 6.79 us -> 2.22 us  [ring(): from_down = lax.ppermute(value, axis, down)]
    pallas_call x1 -> x4, Pallas kernels: 6.76 us -> 10.1 us  [the longest x2 5.02 us: gate(): pl.pallas_call(functools.partial(gate_kernel, own_half), out_shape=jax.Sh...]
    ppermute x2 -> x1, starting transfers between devices: 5.96 us -> 2.78 us  [ring(): far_down = lax.ppermute(from_down[half:], axis, down)]
    ppermute x0 -> x6, waiting for transfers between devices: none -> 2.88 us  [the longest x1 2.86 us: split_ring(): up_low = lax.ppermute(low, axis, up)]
  transfers between devices with their start and end apart: 8 -> 10, of which waited for: 6 -> 4; matrix products, arithmetic and copies ran while one was open for 0% -> 0% of each run, Pallas kernels for 0% -> 8%
where the time goes in v3:
time: 95.2 us; the launch traced here: 94.2 us
  blocking collectives  46.4 us (49%)
  starting transfers between devices  19.6 us (21%)
  waiting for transfers between devices  13.1 us (14%)
  Pallas kernels  12.4 us (13%)
  local copies, waits for them, and re-layouts  2.48 us (3%)
    all_to_all x1, blocking collectives, per_device(): shares = lax.all_to_all(partial_value, ('l', 'y'), 0, 0, tiled=True)  17.3 us
    all_to_all x1, blocking collectives, per_device(): got = lax.all_to_all(spread, ('x', 'l', 'y'), 0, 0, tiled=True)  16.4 us
    all_to_all x1, blocking collectives, per_device(): quarters = lax.all_to_all(routed, ('l', 'y'), 0, 0, tiled=True)  12.6 us
    ppermute x1, waiting for transfers between devices, ring(): from_up = lax.ppermute(value, axis, up)  5.36 us
    pallas_call x2, Pallas kernels, gate(): pl.pallas_call(functools.partial(gate_kernel, own_half), out_shape=jax.Sh...  5.02 us
    ppermute x1, starting transfers between devices, ring(): from_up = lax.ppermute(value, axis, up)  3.35 us
    ppermute x1, starting transfers between devices, split_ring(): far_down = lax.ppermute(down_high, axis, down)  3.24 us
    ppermute x1, starting transfers between devices, split_ring(): down_low = lax.ppermute(low, axis, down)  3.23 us
  transfers between devices with their start and end apart: 10, of which 4 were waited for; matrix products, arithmetic and copies ran while one was open for 0% of the time, Pallas kernels for 8%

profile of v3, /device:TPU:32, one launch (start us, length us, event | category | flops | bytes accessed | tf_op | source)
XLA Modules:
  0.0 94.2 jit_solution(11196772799537144009)
XLA Ops:
  0.0 0.0 copy-start.1
  0.0 0.1 pad_add_fusion.pos_ref
  0.1 0.0 copy-start.3
  0.1 0.9 copy-done.3
  1.0 0.6 spread.1
  1.6 16.4 %all_to_all.19.got_ref = bf16[32,2,16,128]{3,2,1,0:T(8,128)(2,1)S(1)} all-to-all(bf16[32,2,16,128]{3,2,1,0:T(8,128)(2,1)S(1)} %spread.1), channel_id=1, replica_groups=mesh['x'=4,'z'=4,'l'=2,'y'=4,'snode'=2] {'x','l','y'}, dimensions={0} | all-to-all | bytes 524288 | tf_op jit(solution)/shard_map/all_to_all | solution.py:184
  18.0 0.6 compact.1
  18.6 3.3 %collective-permute-start = (bf16[40,16,128]{2,1,0:T(8,128)(2,1)S(1)}, bf16[40,16,128]{2,1,0:T(8,128)(2,1)S(1)}, u32[]{:S(2)}, u32[]{:S(2)}) collective-permute-start(bf16[40,16,128]{2,1,0:T(8,128)(2,1)S(1)} %compact.1), channel_id=1, source_target_pairs={{0,16},{16,32},{32,48},{48,0},{1,17},{17,33},{33,49},{49,1},{2,18}... | collective-permute-start | bytes 491528 | tf_op jit(solution)/shard_map/ppermute | solution.py:143
  22.0 2.2 %collective-permute-start.1 = (bf16[40,16,128]{2,1,0:T(8,128)(2,1)S(1)}, bf16[40,16,128]{2,1,0:T(8,128)(2,1)S(1)}, u32[]{:S(2)}, u32[]{:S(2)}) collective-permute-start(bf16[40,16,128]{2,1,0:T(8,128)(2,1)S(1)} %compact.1), channel_id=1, source_target_pairs={{0,48},{16,0},{32,16},{48,32},{1,49},{17,1},{33,17},{49,33},{2,50}... | collective-permute-start | bytes 491528 | tf_op jit(solution)/shard_map/ppermute | solution.py:144
  24.2 5.4 %collective-permute-done = bf16[40,16,128]{2,1,0:T(8,128)(2,1)S(1)} collective-permute-done((bf16[40,16,128]{2,1,0:T(8,128)(2,1)S(1)}, bf16[40,16,128]{2,1,0:T(8,128)(2,1)S(1)}, u32[]{:S(2)}, u32[]{:S(2)}) %collective-permute-start) | collective-permute-done | bytes 163872 | tf_op jit(solution)/shard_map/ppermute | solution.py:143
  29.6 1.4 %collective-permute-start.2 = (bf16[20,16,128]{2,1,0:T(8,128)(2,1)S(1)}, bf16[20,16,128]{2,1,0:T(8,128)(2,1)S(1)}, u32[]{:S(2)}, u32[]{:S(2)}) collective-permute-start(bf16[20,16,128]{2,1,0:T(8,128)(2,1)S(1)} %slice.16), channel_id=1, source_target_pairs={{0,16},{16,32},{32,48},{48,0},{1,17},{17,33},{33,49},{49,1},{2,18}... | collective-permute-start | bytes 245768 | tf_op jit(solution)/shard_map/ppermute | solution.py:145
  31.0 0.0 collective-permute-done.1
  31.0 0.0 copy-start
  31.0 0.0 copy-start.2
  31.0 2.8 %collective-permute-start.3 = (bf16[20,16,128]{2,1,0:T(8,128)(2,1)S(1)}, bf16[20,16,128]{2,1,0:T(8,128)(2,1)S(1)}, u32[]{:S(2)}, u32[]{:S(2)}) collective-permute-start(bf16[20,16,128]{2,1,0:T(8,128)(2,1)S(1)} %slice.17), channel_id=1, source_target_pairs={{0,48},{16,0},{32,16},{48,32},{1,49},{17,1},{33,17},{49,33},{2,50}... | collective-permute-start | bytes 245768 | tf_op jit(solution)/shard_map/ppermute | solution.py:146
  33.9 2.3 %collective-permute-done.2 = bf16[20,16,128]{2,1,0:T(8,128)(2,1)S(1)} collective-permute-done((bf16[20,16,128]{2,1,0:T(8,128)(2,1)S(1)}, bf16[20,16,128]{2,1,0:T(8,128)(2,1)S(1)}, u32[]{:S(2)}, u32[]{:S(2)}) %collective-permute-start.2) | collective-permute-done | bytes 81952 | tf_op jit(solution)/shard_map/ppermute | solution.py:145
  36.2 2.6 %collective-permute-done.3 = bf16[20,16,128]{2,1,0:T(8,128)(2,1)S(1)} collective-permute-done((bf16[20,16,128]{2,1,0:T(8,128)(2,1)S(1)}, bf16[20,16,128]{2,1,0:T(8,128)(2,1)S(1)}, u32[]{:S(2)}, u32[]{:S(2)}) %collective-permute-start.3) | collective-permute-done | bytes 81952 | tf_op jit(solution)/shard_map/ppermute | solution.py:146
  38.7 0.0 copy-start.4
  38.7 0.7 copy-done.4
  39.4 0.7 route.1
  40.1 12.6 %all_to_all.20 = bf16[80,2,16,128]{3,2,1,0:T(8,128)(2,1)S(1)} all-to-all(bf16[80,2,16,128]{3,2,1,0:T(8,128)(2,1)S(1)} %route.1), channel_id=1, replica_groups=mesh['x'=4,'z'=4,'l'=2,'y'=4,'snode'=2] {'l','y'}, dimensions={0} | all-to-all | bytes 1310720 | tf_op jit(solution)/shard_map/all_to_all | solution.py:218
  52.7 0.0 copy-done.1
  52.7 0.4 normal.1._after.own_ref
  53.2 0.1 collective-permute-start.4
  53.3 3.2 %collective-permute-start.5 = (bf16[320,512]{1,0:T(8,128)(2,1)S(1)}, bf16[320,512]{1,0:T(8,128)(2,1)S(1)}, u32[]{:S(2)}, u32[]{:S(2)}) collective-permute-start(bf16[320,512]{1,0:T(8,128)(2,1)S(1)} %get-tuple-element.11), channel_id=1, source_target_pairs={{0,192},{64,0},{128,64},{192,128},{1,193},{65,1},{129,65},{193,129... | collective-permute-start | bytes 983048 | tf_op jit(solution)/shard_map/ppermute | solution.py:157
  56.5 0.0 collective-permute-start.6
  56.5 3.2 %collective-permute-start.7 = (bf16[320,512]{1,0:T(8,128)(2,1)S(1)}, bf16[320,512]{1,0:T(8,128)(2,1)S(1)}, u32[]{:S(2)}, u32[]{:S(2)}) collective-permute-start(bf16[320,512]{1,0:T(8,128)(2,1)S(1)} %get-tuple-element.12), channel_id=1, source_target_pairs={{0,192},{64,0},{128,64},{192,128},{1,193},{65,1},{129,65},{193,129... | collective-permute-start | bytes 983048 | tf_op jit(solution)/shard_map/ppermute | solution.py:159
  59.7 0.0 copy-done
  59.7 0.0 copy-done.2
  59.7 2.5 %gate.2.a_ref = bf16[1280,1280]{1,0:T(8,128)(2,1)S(1)} custom-call(s32[4]{0:T(128)S(1)} %pad_add_fusion.pos_ref, s32[80,80]{1,0:T(8,128)S(1)} %copy-done.2, bf16[1280,2560]{1,0:T(8,128)(2,1)S(1)} %copy-done, bf16[640,512]{1,0:T(8,128)(2,1)S(1)} %normal.1._after.own_ref), custom_call_target="tpu_custom_call" | custom-call | flops 1638400 | bytes 6553600 | tf_op jit(solution)/shard_map/gate/pallas_call | solution.py:196
  62.3 2.9 %collective-permute-done.4.ul_ref = bf16[320,512]{1,0:T(8,128)(2,1)S(1)} collective-permute-done((bf16[320,512]{1,0:T(8,128)(2,1)S(1)}, bf16[320,512]{1,0:T(8,128)(2,1)S(1)}, u32[]{:S(2)}, u32[]{:S(2)}) %collective-permute-start.4) | collective-permute-done | bytes 327712 | tf_op jit(solution)/shard_map/ppermute | solution.py:156
  65.1 0.0 collective-permute-done.5.dh_ref
  65.1 0.0 collective-permute-start.8
  65.1 3.2 %collective-permute-start.9 = (bf16[320,512]{1,0:T(8,128)(2,1)S(1)}, bf16[320,512]{1,0:T(8,128)(2,1)S(1)}, u32[]{:S(2)}, u32[]{:S(2)}) collective-permute-start(bf16[320,512]{1,0:T(8,128)(2,1)S(1)} %collective-permute-done.5.dh_ref), channel_id=1, source_target_pairs={{0,192},{64,0},{128,64},{192,128},{1,193},{65,1},{129,65},{193,129... | collective-permute-start | bytes 983048 | tf_op jit(solution)/shard_map/ppermute | solution.py:162
  68.4 2.5 %gate.3.a_ref = bf16[1280,1280]{1,0:T(8,128)(2,1)S(1)} custom-call(s32[4]{0:T(128)S(1)} %pad_add_fusion.pos_ref, s32[80,80]{1,0:T(8,128)S(1)} %copy-done.2, bf16[1280,2560]{1,0:T(8,128)(2,1)S(1)} %copy-done, bf16[640,512]{1,0:T(8,128)(2,1)S(1)} %normal.1._after.own_ref), custom_call_target="tpu_custom_call" | custom-call | flops 1638400 | bytes 6553600 | tf_op jit(solution)/shard_map/gate/pallas_call | solution.py:196
  70.9 0.0 collective-permute-done.6.uh_ref
  70.9 0.0 collective-permute-done.7.dl_ref
  70.9 2.5 %near.1.near_ref = f32[1280,512]{1,0:T(8,128)S(1)} custom-call(s32[4]{0:T(128)S(1)} %pad_add_fusion.pos_ref, bf16[1280,1280]{1,0:T(8,128)(2,1)S(1)} %gate.3.a_ref, bf16[320,512]{1,0:T(8,128)(2,1)S(1)} %collective-permute-done.4.ul_ref, bf16[320,512]{1,0:T(8,128)(2,1)S(1)} %collective-permute-done.6.uh_ref, ...), custom_call_target="tpu_custom_call" | custom-call | flops 1677721600 | tf_op jit(solution)/shard_map/near/pallas_call | solution.py:230
  73.4 0.0 collective-permute-done.8.fu_ref
  73.4 0.0 collective-permute-done.9.fd_ref
  73.4 2.6 %far.1 = bf16[1280,512]{1,0:T(8,128)(2,1)S(1)} custom-call(s32[4]{0:T(128)S(1)} %pad_add_fusion.pos_ref, bf16[1280,1280]{1,0:T(8,128)(2,1)S(1)} %gate.2.a_ref, f32[1280,512]{1,0:T(8,128)S(1)} %near.1.near_ref, bf16[640,512]{1,0:T(8,128)(2,1)S(1)} %normal.1._after.own_ref, bf16[320,512]{1,0:T(8,128)(2,1)S(1)} %collective-permute-done.8.fu_ref, ...), custom_call_target="tpu_custom_call" | custom-call | tf_op jit(solution)/shard_map/far/pallas_call | solution.py:242
  76.0 17.3 %all_to_all.21 = bf16[8,160,512]{2,1,0:T(8,128)(2,1)S(1)} all-to-all(bf16[8,160,512]{2,1,0:T(8,128)(2,1)S(1)} %bitcast.7), channel_id=1, replica_groups=mesh['x'=4,'z'=4,'l'=2,'y'=4,'snode'=2] {'l','y'}, dimensions={0} | all-to-all | bytes 2621440 | tf_op jit(solution)/shard_map/all_to_all | solution.py:252
  93.3 0.2 reduce_sum.12
  93.5 0.7 copy.6
  (9 shorter events, 0.2 us)
Async XLA Ops:
  0.0 52.7 %copy-start.1 = (bf16[2,256,256]{2,1,0:T(8,128)(2,1)S(1)}, bf16[2,256,256]{2,1,0:T(8,128)(2,1)}, u32[]{:S(2)}) copy-start(bf16[2,256,256]{2,1,0:T(8,128)(2,1)} %diag_ref.1) | copy-start | bytes 786436
  0.1 0.9 copy-start.3
  18.6 10.9 %collective-permute-start = (bf16[40,16,128]{2,1,0:T(8,128)(2,1)S(1)}, bf16[40,16,128]{2,1,0:T(8,128)(2,1)S(1)}, u32[]{:S(2)}, u32[]{:S(2)}) collective-permute-start(bf16[40,16,128]{2,1,0:T(8,128)(2,1)S(1)} %compact.1), channel_id=1, source_target_pairs={{0,16},{16,32},{32,48},{48,0},{1,17},{17,33},{33,49},{49,1},{2,18}... | collective-permute-start | bytes 491528 | tf_op jit(solution)/shard_map/ppermute | solution.py:143
  22.0 9.0 %collective-permute-start.1 = (bf16[40,16,128]{2,1,0:T(8,128)(2,1)S(1)}, bf16[40,16,128]{2,1,0:T(8,128)(2,1)S(1)}, u32[]{:S(2)}, u32[]{:S(2)}) collective-permute-start(bf16[40,16,128]{2,1,0:T(8,128)(2,1)S(1)} %compact.1), channel_id=1, source_target_pairs={{0,48},{16,0},{32,16},{48,32},{1,49},{17,1},{33,17},{49,33},{2,50}... | collective-permute-start | bytes 491528 | tf_op jit(solution)/shard_map/ppermute | solution.py:144
  29.6 6.6 %collective-permute-start.2 = (bf16[20,16,128]{2,1,0:T(8,128)(2,1)S(1)}, bf16[20,16,128]{2,1,0:T(8,128)(2,1)S(1)}, u32[]{:S(2)}, u32[]{:S(2)}) collective-permute-start(bf16[20,16,128]{2,1,0:T(8,128)(2,1)S(1)} %slice.16), channel_id=1, source_target_pairs={{0,16},{16,32},{32,48},{48,0},{1,17},{17,33},{33,49},{49,1},{2,18}... | collective-permute-start | bytes 245768 | tf_op jit(solution)/shard_map/ppermute | solution.py:145
  31.0 28.7 %copy-start = (bf16[1280,2560]{1,0:T(8,128)(2,1)S(1)}, bf16[1280,2560]{1,0:T(8,128)(2,1)}, u32[]{:S(2)}) copy-start(bf16[1280,2560]{1,0:T(8,128)(2,1)} %a_ref.3) | copy-start | bytes 19660804
  31.0 28.7 %copy-start.2 = (s32[80,80]{1,0:T(8,128)S(1)}, s32[80,80]{1,0:T(8,128)}, u32[]{:S(2)}) copy-start(s32[80,80]{1,0:T(8,128)} %mask_ref.3) | copy-start | bytes 76804
  31.0 7.7 %collective-permute-start.3 = (bf16[20,16,128]{2,1,0:T(8,128)(2,1)S(1)}, bf16[20,16,128]{2,1,0:T(8,128)(2,1)S(1)}, u32[]{:S(2)}, u32[]{:S(2)}) collective-permute-start(bf16[20,16,128]{2,1,0:T(8,128)(2,1)S(1)} %slice.17), channel_id=1, source_target_pairs={{0,48},{16,0},{32,16},{48,32},{1,49},{17,1},{33,17},{49,33},{2,50}... | collective-permute-start | bytes 245768 | tf_op jit(solution)/shard_map/ppermute | solution.py:146
  38.7 0.7 copy-start.4
  53.2 11.9 %collective-permute-start.4 = (bf16[320,512]{1,0:T(8,128)(2,1)S(1)}, bf16[320,512]{1,0:T(8,128)(2,1)S(1)}, u32[]{:S(2)}, u32[]{:S(2)}) collective-permute-start(bf16[320,512]{1,0:T(8,128)(2,1)S(1)} %get-tuple-element.12), channel_id=1, source_target_pairs={{0,64},{64,128},{128,192},{192,0},{1,65},{65,129},{129,193},{193,1... | collective-permute-start | bytes 983048 | tf_op jit(solution)/shard_map/ppermute | solution.py:156
  53.3 11.8 %collective-permute-start.5 = (bf16[320,512]{1,0:T(8,128)(2,1)S(1)}, bf16[320,512]{1,0:T(8,128)(2,1)S(1)}, u32[]{:S(2)}, u32[]{:S(2)}) collective-permute-start(bf16[320,512]{1,0:T(8,128)(2,1)S(1)} %get-tuple-element.11), channel_id=1, source_target_pairs={{0,192},{64,0},{128,64},{192,128},{1,193},{65,1},{129,65},{193,129... | collective-permute-start | bytes 983048 | tf_op jit(solution)/shard_map/ppermute | solution.py:157
  56.5 14.4 %collective-permute-start.6 = (bf16[320,512]{1,0:T(8,128)(2,1)S(1)}, bf16[320,512]{1,0:T(8,128)(2,1)S(1)}, u32[]{:S(2)}, u32[]{:S(2)}) collective-permute-start(bf16[320,512]{1,0:T(8,128)(2,1)S(1)} %get-tuple-element.11), channel_id=1, source_target_pairs={{0,64},{64,128},{128,192},{192,0},{1,65},{65,129},{129,193},{193,1... | collective-permute-start | bytes 983048 | tf_op jit(solution)/shard_map/ppermute | solution.py:158
  56.5 14.4 %collective-permute-start.7 = (bf16[320,512]{1,0:T(8,128)(2,1)S(1)}, bf16[320,512]{1,0:T(8,128)(2,1)S(1)}, u32[]{:S(2)}, u32[]{:S(2)}) collective-permute-start(bf16[320,512]{1,0:T(8,128)(2,1)S(1)} %get-tuple-element.12), channel_id=1, source_target_pairs={{0,192},{64,0},{128,64},{192,128},{1,193},{65,1},{129,65},{193,129... | collective-permute-start | bytes 983048 | tf_op jit(solution)/shard_map/ppermute | solution.py:159
  65.1 8.3 %collective-permute-start.8 = (bf16[320,512]{1,0:T(8,128)(2,1)S(1)}, bf16[320,512]{1,0:T(8,128)(2,1)S(1)}, u32[]{:S(2)}, u32[]{:S(2)}) collective-permute-start(bf16[320,512]{1,0:T(8,128)(2,1)S(1)} %collective-permute-done.4.ul_ref), channel_id=1, source_target_pairs={{0,64},{64,128},{128,192},{192,0},{1,65},{65,129},{129,193},{193,1... | collective-permute-start | bytes 983048 | tf_op jit(solution)/shard_map/ppermute | solution.py:161
  65.1 8.3 %collective-permute-start.9 = (bf16[320,512]{1,0:T(8,128)(2,1)S(1)}, bf16[320,512]{1,0:T(8,128)(2,1)S(1)}, u32[]{:S(2)}, u32[]{:S(2)}) collective-permute-start(bf16[320,512]{1,0:T(8,128)(2,1)S(1)} %collective-permute-done.5.dh_ref), channel_id=1, source_target_pairs={{0,192},{64,0},{128,64},{192,128},{1,193},{65,1},{129,65},{193,129... | collective-permute-start | bytes 983048 | tf_op jit(solution)/shard_map/ppermute | solution.py:162

commit v4 on v3

--- a/solution.py
+++ b/solution.py
@@ -40,7 +40,7 @@
                 out_ref[slot, s] = l_ref[s, i * SLICE : (i + 1) * SLICE, l * LANES : (l + 1) * LANES]
 
 
-def compact_kernel(pos_ref, got_ref, out_ref):
+def compact_kernel(pos_ref, _order, got_ref, out_ref):
     snodes = got_ref.shape[1]
     per_row = out_ref.shape[0] // (NX * snodes)
     count = per_row * NX * NY // (NL * NY)
@@ -115,8 +115,9 @@
             out_ref[down, at] = out_ref[down, at] * keep.astype(jnp.bfloat16)
 
 
-def near_kernel(pos_ref, a_ref, ul_ref, uh_ref, dl_ref, dh_ref, out_ref, stacked):
+def near_kernel(pos_ref, a_ref, own_ref, ul_ref, uh_ref, dl_ref, dh_ref, out_ref, begun_ref, stacked):
     x = pos_ref[0]
+    fill(begun_ref, ((x, (own_ref,)),))
     fill(stacked, (((x - 1) & (NX - 1), (ul_ref, uh_ref)), ((x + 1) & (NX - 1), (dl_ref, dh_ref))))
     tile = 2 * LANES
     for n in range(out_ref.shape[1] // tile):
@@ -124,9 +125,9 @@
         out_ref[:, at] = jnp.dot(a_ref[...], stacked[:, at], preferred_element_type=jnp.float32)
 
 
-def far_kernel(pos_ref, a_ref, near_ref, own_ref, fu_ref, fd_ref, out_ref, stacked):
+def far_kernel(pos_ref, a_ref, near_ref, _, fu_ref, fd_ref, out_ref, stacked):
     x = pos_ref[0]
-    fill(stacked, ((x, (own_ref,)), ((x + 2) & (NX - 1), (fu_ref, fd_ref))))
+    fill(stacked, (((x + 2) & (NX - 1), (fu_ref, fd_ref)),))
     tile = 2 * LANES
     for n in range(out_ref.shape[1] // tile):
         at = slice(n * tile, (n + 1) * tile)
@@ -185,11 +186,11 @@
     mine = pl.pallas_call(
         compact_kernel,
         out_shape=jax.ShapeDtypeStruct((blocks // NZ * snodes, SLICE, LANES), bf16),
-        in_specs=[whole(SMEM), whole()],
+        in_specs=[whole(SMEM), whole(pl.ANY), whole()],
         out_specs=whole(),
         compiler_params=params(),
         name="compact",
-    )(pos, got)
+    )(pos, block_order, got)
     half_cols = local_cols // 2
 
     def gate(own_half, after):
@@ -227,27 +228,33 @@
     )(quarters.reshape(cols, share, snodes, SLICE, LANES), diag_inverse)
     (own, *near, far_up, far_down), gated_own = split_ring(own, "x", lambda: gate(True, own))
     gated_other = gate(False, own)
-    near_value = pl.pallas_call(
+    near_value, begun = pl.pallas_call(
         near_kernel,
-        out_shape=jax.ShapeDtypeStruct((local_rows, width), jnp.float32),
-        in_specs=[whole(SMEM)] + [whole()] * 5,
-        out_specs=whole(),
+        out_shape=(
+            jax.ShapeDtypeStruct((local_rows, width), jnp.float32),
+            jax.ShapeDtypeStruct((half_cols, width), bf16),
+        ),
+        in_specs=[whole(SMEM)] + [whole()] * 6,
+        out_specs=(whole(), whole()),
         scratch_shapes=[VMEM((half_cols, width), bf16)],
         compiler_params=params(),
         cost_estimate=pl.CostEstimate(
             flops=local_rows * local_cols * width, bytes_accessed=0, transcendentals=0
         ),
         name="near",
-    )(pos, gated_other, *near)
-    partial_value = pl.pallas_call(
+    )(pos, gated_other, own, *near)
+    partial_value, _ = pl.pallas_call(
         far_kernel,
-        out_shape=jax.ShapeDtypeStruct((local_rows, width), bf16),
+        out_shape=(
+            jax.ShapeDtypeStruct((local_rows, width), bf16),
+            jax.ShapeDtypeStruct((half_cols, width), bf16),
+        ),
         in_specs=[whole(SMEM)] + [whole()] * 5,
-        out_specs=whole(),
-        scratch_shapes=[VMEM((half_cols, width), bf16)],
+        out_specs=(whole(), whole()),
+        input_output_aliases={3: 1},
         compiler_params=params(),
         name="far",
-    )(pos, gated_own, near_value, own, far_up, far_down)
+    )(pos, gated_own, near_value, begun, far_up, far_down)
     share_rows = local_rows // cols
     shares = lax.all_to_all(partial_value, ("l", "y"), 0, 0, tiled=True)
     summed = shares.reshape(cols, share_rows, snodes, tile).astype(jnp.float32).sum(0)

time: 95.2 us -> 95.3 us (level)
  no operation moved by 1% of the time
where the time goes in v4:
time: 95.3 us; the launch traced here: 94.4 us
  blocking collectives  46.5 us (49%)
  starting transfers between devices  19.6 us (21%)
  waiting for transfers between devices  13.1 us (14%)
  Pallas kernels  12.4 us (13%)
  local copies, waits for them, and re-layouts  2.49 us (3%)
    all_to_all x1, blocking collectives, per_device(): shares = lax.all_to_all(partial_value, ('l', 'y'), 0, 0, tiled=True)  17.3 us
    all_to_all x1, blocking collectives, per_device(): got = lax.all_to_all(spread, ('x', 'l', 'y'), 0, 0, tiled=True)  16.5 us
    all_to_all x1, blocking collectives, per_device(): quarters = lax.all_to_all(routed, ('l', 'y'), 0, 0, tiled=True)  12.6 us
    ppermute x1, waiting for transfers between devices, ring(): from_up = lax.ppermute(value, axis, up)  5.36 us
    pallas_call x2, Pallas kernels, gate(): pl.pallas_call(functools.partial(gate_kernel, own_half), out_shape=jax.Sh...  5.02 us
    ppermute x1, starting transfers between devices, ring(): from_up = lax.ppermute(value, axis, up)  3.35 us
    ppermute x1, starting transfers between devices, split_ring(): far_down = lax.ppermute(down_high, axis, down)  3.24 us
    ppermute x1, starting transfers between devices, split_ring(): down_low = lax.ppermute(low, axis, down)  3.23 us
  transfers between devices with their start and end apart: 10, of which 4 were waited for; matrix products, arithmetic and copies ran while one was open for 0% of the time, Pallas kernels for 8%

profile of v4, /device:TPU:32, one launch (start us, length us, event | category | flops | bytes accessed | tf_op | source)
XLA Modules:
  0.0 94.4 jit_solution(12199484903966171917)
XLA Ops:
  0.0 0.1 pad_add_fusion.pos_ref
  0.1 0.0 copy-start.3
  0.1 0.9 copy-done.3
  1.0 0.6 spread.1
  1.6 0.0 copy-start.1
  1.6 16.5 %all_to_all.19.got_ref = bf16[32,2,16,128]{3,2,1,0:T(8,128)(2,1)S(1)} all-to-all(bf16[32,2,16,128]{3,2,1,0:T(8,128)(2,1)S(1)} %spread.1), channel_id=1, replica_groups=mesh['x'=4,'z'=4,'l'=2,'y'=4,'snode'=2] {'x','l','y'}, dimensions={0} | all-to-all | bytes 524288 | tf_op jit(solution)/shard_map/all_to_all | solution.py:185
  18.2 0.0 copy-start.4
  18.2 0.7 copy-done.4
  18.9 0.6 compact.1
  19.5 3.3 %collective-permute-start = (bf16[40,16,128]{2,1,0:T(8,128)(2,1)S(1)}, bf16[40,16,128]{2,1,0:T(8,128)(2,1)S(1)}, u32[]{:S(2)}, u32[]{:S(2)}) collective-permute-start(bf16[40,16,128]{2,1,0:T(8,128)(2,1)S(1)} %compact.1), channel_id=1, source_target_pairs={{0,16},{16,32},{32,48},{48,0},{1,17},{17,33},{33,49},{49,1},{2,18}... | collective-permute-start | bytes 491528 | tf_op jit(solution)/shard_map/ppermute | solution.py:144
  22.8 2.2 %collective-permute-start.1 = (bf16[40,16,128]{2,1,0:T(8,128)(2,1)S(1)}, bf16[40,16,128]{2,1,0:T(8,128)(2,1)S(1)}, u32[]{:S(2)}, u32[]{:S(2)}) collective-permute-start(bf16[40,16,128]{2,1,0:T(8,128)(2,1)S(1)} %compact.1), channel_id=1, source_target_pairs={{0,48},{16,0},{32,16},{48,32},{1,49},{17,1},{33,17},{49,33},{2,50}... | collective-permute-start | bytes 491528 | tf_op jit(solution)/shard_map/ppermute | solution.py:145
  25.0 5.4 %collective-permute-done = bf16[40,16,128]{2,1,0:T(8,128)(2,1)S(1)} collective-permute-done((bf16[40,16,128]{2,1,0:T(8,128)(2,1)S(1)}, bf16[40,16,128]{2,1,0:T(8,128)(2,1)S(1)}, u32[]{:S(2)}, u32[]{:S(2)}) %collective-permute-start) | collective-permute-done | bytes 163872 | tf_op jit(solution)/shard_map/ppermute | solution.py:144
  30.4 1.4 %collective-permute-start.2 = (bf16[20,16,128]{2,1,0:T(8,128)(2,1)S(1)}, bf16[20,16,128]{2,1,0:T(8,128)(2,1)S(1)}, u32[]{:S(2)}, u32[]{:S(2)}) collective-permute-start(bf16[20,16,128]{2,1,0:T(8,128)(2,1)S(1)} %slice.16), channel_id=1, source_target_pairs={{0,16},{16,32},{32,48},{48,0},{1,17},{17,33},{33,49},{49,1},{2,18}... | collective-permute-start | bytes 245768 | tf_op jit(solution)/shard_map/ppermute | solution.py:146
  31.8 0.0 collective-permute-done.1
  31.8 0.0 copy-start
  31.9 2.8 %collective-permute-start.3 = (bf16[20,16,128]{2,1,0:T(8,128)(2,1)S(1)}, bf16[20,16,128]{2,1,0:T(8,128)(2,1)S(1)}, u32[]{:S(2)}, u32[]{:S(2)}) collective-permute-start(bf16[20,16,128]{2,1,0:T(8,128)(2,1)S(1)} %slice.17), channel_id=1, source_target_pairs={{0,48},{16,0},{32,16},{48,32},{1,49},{17,1},{33,17},{49,33},{2,50}... | collective-permute-start | bytes 245768 | tf_op jit(solution)/shard_map/ppermute | solution.py:147
  34.7 2.3 %collective-permute-done.2 = bf16[20,16,128]{2,1,0:T(8,128)(2,1)S(1)} collective-permute-done((bf16[20,16,128]{2,1,0:T(8,128)(2,1)S(1)}, bf16[20,16,128]{2,1,0:T(8,128)(2,1)S(1)}, u32[]{:S(2)}, u32[]{:S(2)}) %collective-permute-start.2) | collective-permute-done | bytes 81952 | tf_op jit(solution)/shard_map/ppermute | solution.py:146
  37.0 2.5 %collective-permute-done.3 = bf16[20,16,128]{2,1,0:T(8,128)(2,1)S(1)} collective-permute-done((bf16[20,16,128]{2,1,0:T(8,128)(2,1)S(1)}, bf16[20,16,128]{2,1,0:T(8,128)(2,1)S(1)}, u32[]{:S(2)}, u32[]{:S(2)}) %collective-permute-start.3) | collective-permute-done | bytes 81952 | tf_op jit(solution)/shard_map/ppermute | solution.py:147
  39.5 0.0 copy-start.2
  39.6 0.7 route.1
  40.3 12.6 %all_to_all.20 = bf16[80,2,16,128]{3,2,1,0:T(8,128)(2,1)S(1)} all-to-all(bf16[80,2,16,128]{3,2,1,0:T(8,128)(2,1)S(1)} %route.1), channel_id=1, replica_groups=mesh['x'=4,'z'=4,'l'=2,'y'=4,'snode'=2] {'l','y'}, dimensions={0} | all-to-all | bytes 1310720 | tf_op jit(solution)/shard_map/all_to_all | solution.py:219
  52.9 0.0 copy-done.1
  52.9 0.4 normal.1._after.own_ref
  53.3 0.1 collective-permute-start.4
  53.4 3.2 %collective-permute-start.5 = (bf16[320,512]{1,0:T(8,128)(2,1)S(1)}, bf16[320,512]{1,0:T(8,128)(2,1)S(1)}, u32[]{:S(2)}, u32[]{:S(2)}) collective-permute-start(bf16[320,512]{1,0:T(8,128)(2,1)S(1)} %get-tuple-element.17), channel_id=1, source_target_pairs={{0,192},{64,0},{128,64},{192,128},{1,193},{65,1},{129,65},{193,129... | collective-permute-start | bytes 983048 | tf_op jit(solution)/shard_map/ppermute | solution.py:158
  56.6 0.0 collective-permute-start.6
  56.6 3.2 %collective-permute-start.7 = (bf16[320,512]{1,0:T(8,128)(2,1)S(1)}, bf16[320,512]{1,0:T(8,128)(2,1)S(1)}, u32[]{:S(2)}, u32[]{:S(2)}) collective-permute-start(bf16[320,512]{1,0:T(8,128)(2,1)S(1)} %get-tuple-element.18), channel_id=1, source_target_pairs={{0,192},{64,0},{128,64},{192,128},{1,193},{65,1},{129,65},{193,129... | collective-permute-start | bytes 983048 | tf_op jit(solution)/shard_map/ppermute | solution.py:160
  59.9 0.0 copy-done
  59.9 0.0 copy-done.2
  59.9 2.5 %gate.2.a_ref = bf16[1280,1280]{1,0:T(8,128)(2,1)S(1)} custom-call(s32[4]{0:T(128)S(1)} %pad_add_fusion.pos_ref, s32[80,80]{1,0:T(8,128)S(1)} %copy-done.2, bf16[1280,2560]{1,0:T(8,128)(2,1)S(1)} %copy-done, bf16[640,512]{1,0:T(8,128)(2,1)S(1)} %normal.1._after.own_ref), custom_call_target="tpu_custom_call" | custom-call | flops 1638400 | bytes 6553600 | tf_op jit(solution)/shard_map/gate/pallas_call | solution.py:197
  62.4 2.9 %collective-permute-done.4.ul_ref = bf16[320,512]{1,0:T(8,128)(2,1)S(1)} collective-permute-done((bf16[320,512]{1,0:T(8,128)(2,1)S(1)}, bf16[320,512]{1,0:T(8,128)(2,1)S(1)}, u32[]{:S(2)}, u32[]{:S(2)}) %collective-permute-start.4) | collective-permute-done | bytes 327712 | tf_op jit(solution)/shard_map/ppermute | solution.py:157
  65.3 0.0 collective-permute-done.5.dh_ref
  65.3 0.0 collective-permute-start.8
  65.3 3.2 %collective-permute-start.9 = (bf16[320,512]{1,0:T(8,128)(2,1)S(1)}, bf16[320,512]{1,0:T(8,128)(2,1)S(1)}, u32[]{:S(2)}, u32[]{:S(2)}) collective-permute-start(bf16[320,512]{1,0:T(8,128)(2,1)S(1)} %collective-permute-done.5.dh_ref), channel_id=1, source_target_pairs={{0,192},{64,0},{128,64},{192,128},{1,193},{65,1},{129,65},{193,129... | collective-permute-start | bytes 983048 | tf_op jit(solution)/shard_map/ppermute | solution.py:163
  68.5 2.5 %gate.3.a_ref = bf16[1280,1280]{1,0:T(8,128)(2,1)S(1)} custom-call(s32[4]{0:T(128)S(1)} %pad_add_fusion.pos_ref, s32[80,80]{1,0:T(8,128)S(1)} %copy-done.2, bf16[1280,2560]{1,0:T(8,128)(2,1)S(1)} %copy-done, bf16[640,512]{1,0:T(8,128)(2,1)S(1)} %normal.1._after.own_ref), custom_call_target="tpu_custom_call" | custom-call | flops 1638400 | bytes 6553600 | tf_op jit(solution)/shard_map/gate/pallas_call | solution.py:197
  71.0 0.0 collective-permute-done.6.uh_ref
  71.0 0.0 collective-permute-done.7.dl_ref
  71.0 2.5 %near.1 = (f32[1280,512]{1,0:T(8,128)S(1)}, bf16[1280,512]{1,0:T(8,128)(2,1)S(1)}) custom-call(s32[4]{0:T(128)S(1)} %pad_add_fusion.pos_ref, bf16[1280,1280]{1,0:T(8,128)(2,1)S(1)} %gate.3.a_ref, bf16[640,512]{1,0:T(8,128)(2,1)S(1)} %normal.1._after.own_ref, bf16[320,512]{1,0:T(8,128)(2,1)S(1)} %collective-permute-done.4.ul_ref, ...), custom_call_target="tpu_custom_call" | custom-call | flops 1677721600 | tf_op jit(solution)/shard_map/near/pallas_call | solution.py:231
  73.6 0.0 collective-permute-done.8.fu_ref
  73.6 0.0 collective-permute-done.9.fd_ref
  73.6 2.5 %far.1 = (bf16[1280,512]{1,0:T(8,128)(2,1)S(1)}, bf16[1280,512]{1,0:T(8,128)(2,1)S(1)}) custom-call(s32[4]{0:T(128)S(1)} %pad_add_fusion.pos_ref, bf16[1280,1280]{1,0:T(8,128)(2,1)S(1)} %gate.2.a_ref, f32[1280,512]{1,0:T(8,128)S(1)} %get-tuple-element.14.near_ref, bf16[1280,512]{1,0:T(8,128)(2,1)S(1)} %get-tuple-element.15._, ...), custom_call_target="tpu_custom_call", output_to_operand_aliasing={{1}: (3, {})} | custom-call | tf_op jit(solution)/shard_map/far/pallas_call | solution.py:246
  76.1 17.3 %all_to_all.21 = bf16[8,160,512]{2,1,0:T(8,128)(2,1)S(1)} all-to-all(bf16[8,160,512]{2,1,0:T(8,128)(2,1)S(1)} %bitcast.8), channel_id=1, replica_groups=mesh['x'=4,'z'=4,'l'=2,'y'=4,'snode'=2] {'l','y'}, dimensions={0} | all-to-all | bytes 2621440 | tf_op jit(solution)/shard_map/all_to_all | solution.py:259
  93.4 0.2 reduce_sum.12
  93.7 0.7 copy.7
  (9 shorter events, 0.2 us)
Async XLA Ops:
  0.1 0.9 copy-start.3
  1.6 51.3 %copy-start.1 = (bf16[2,256,256]{2,1,0:T(8,128)(2,1)S(1)}, bf16[2,256,256]{2,1,0:T(8,128)(2,1)}, u32[]{:S(2)}) copy-start(bf16[2,256,256]{2,1,0:T(8,128)(2,1)} %diag_ref.1) | copy-start | bytes 786436
  18.2 0.7 copy-start.4
  19.5 10.9 %collective-permute-start = (bf16[40,16,128]{2,1,0:T(8,128)(2,1)S(1)}, bf16[40,16,128]{2,1,0:T(8,128)(2,1)S(1)}, u32[]{:S(2)}, u32[]{:S(2)}) collective-permute-start(bf16[40,16,128]{2,1,0:T(8,128)(2,1)S(1)} %compact.1), channel_id=1, source_target_pairs={{0,16},{16,32},{32,48},{48,0},{1,17},{17,33},{33,49},{49,1},{2,18}... | collective-permute-start | bytes 491528 | tf_op jit(solution)/shard_map/ppermute | solution.py:144
  22.8 9.0 %collective-permute-start.1 = (bf16[40,16,128]{2,1,0:T(8,128)(2,1)S(1)}, bf16[40,16,128]{2,1,0:T(8,128)(2,1)S(1)}, u32[]{:S(2)}, u32[]{:S(2)}) collective-permute-start(bf16[40,16,128]{2,1,0:T(8,128)(2,1)S(1)} %compact.1), channel_id=1, source_target_pairs={{0,48},{16,0},{32,16},{48,32},{1,49},{17,1},{33,17},{49,33},{2,50}... | collective-permute-start | bytes 491528 | tf_op jit(solution)/shard_map/ppermute | solution.py:145
  30.4 6.6 %collective-permute-start.2 = (bf16[20,16,128]{2,1,0:T(8,128)(2,1)S(1)}, bf16[20,16,128]{2,1,0:T(8,128)(2,1)S(1)}, u32[]{:S(2)}, u32[]{:S(2)}) collective-permute-start(bf16[20,16,128]{2,1,0:T(8,128)(2,1)S(1)} %slice.16), channel_id=1, source_target_pairs={{0,16},{16,32},{32,48},{48,0},{1,17},{17,33},{33,49},{49,1},{2,18}... | collective-permute-start | bytes 245768 | tf_op jit(solution)/shard_map/ppermute | solution.py:146
  31.8 28.0 %copy-start = (bf16[1280,2560]{1,0:T(8,128)(2,1)S(1)}, bf16[1280,2560]{1,0:T(8,128)(2,1)}, u32[]{:S(2)}) copy-start(bf16[1280,2560]{1,0:T(8,128)(2,1)} %a_ref.3) | copy-start | bytes 19660804
  31.9 7.7 %collective-permute-start.3 = (bf16[20,16,128]{2,1,0:T(8,128)(2,1)S(1)}, bf16[20,16,128]{2,1,0:T(8,128)(2,1)S(1)}, u32[]{:S(2)}, u32[]{:S(2)}) collective-permute-start(bf16[20,16,128]{2,1,0:T(8,128)(2,1)S(1)} %slice.17), channel_id=1, source_target_pairs={{0,48},{16,0},{32,16},{48,32},{1,49},{17,1},{33,17},{49,33},{2,50}... | collective-permute-start | bytes 245768 | tf_op jit(solution)/shard_map/ppermute | solution.py:147
  39.5 20.3 %copy-start.2 = (s32[80,80]{1,0:T(8,128)S(1)}, s32[80,80]{1,0:T(8,128)}, u32[]{:S(2)}) copy-start(s32[80,80]{1,0:T(8,128)} %mask_ref.3) | copy-start | bytes 76804
  53.3 11.9 %collective-permute-start.4 = (bf16[320,512]{1,0:T(8,128)(2,1)S(1)}, bf16[320,512]{1,0:T(8,128)(2,1)S(1)}, u32[]{:S(2)}, u32[]{:S(2)}) collective-permute-start(bf16[320,512]{1,0:T(8,128)(2,1)S(1)} %get-tuple-element.18), channel_id=1, source_target_pairs={{0,64},{64,128},{128,192},{192,0},{1,65},{65,129},{129,193},{193,1... | collective-permute-start | bytes 983048 | tf_op jit(solution)/shard_map/ppermute | solution.py:157
  53.4 11.8 %collective-permute-start.5 = (bf16[320,512]{1,0:T(8,128)(2,1)S(1)}, bf16[320,512]{1,0:T(8,128)(2,1)S(1)}, u32[]{:S(2)}, u32[]{:S(2)}) collective-permute-start(bf16[320,512]{1,0:T(8,128)(2,1)S(1)} %get-tuple-element.17), channel_id=1, source_target_pairs={{0,192},{64,0},{128,64},{192,128},{1,193},{65,1},{129,65},{193,129... | collective-permute-start | bytes 983048 | tf_op jit(solution)/shard_map/ppermute | solution.py:158
  56.6 14.4 %collective-permute-start.6 = (bf16[320,512]{1,0:T(8,128)(2,1)S(1)}, bf16[320,512]{1,0:T(8,128)(2,1)S(1)}, u32[]{:S(2)}, u32[]{:S(2)}) collective-permute-start(bf16[320,512]{1,0:T(8,128)(2,1)S(1)} %get-tuple-element.17), channel_id=1, source_target_pairs={{0,64},{64,128},{128,192},{192,0},{1,65},{65,129},{129,193},{193,1... | collective-permute-start | bytes 983048 | tf_op jit(solution)/shard_map/ppermute | solution.py:159
  56.6 14.4 %collective-permute-start.7 = (bf16[320,512]{1,0:T(8,128)(2,1)S(1)}, bf16[320,512]{1,0:T(8,128)(2,1)S(1)}, u32[]{:S(2)}, u32[]{:S(2)}) collective-permute-start(bf16[320,512]{1,0:T(8,128)(2,1)S(1)} %get-tuple-element.18), channel_id=1, source_target_pairs={{0,192},{64,0},{128,64},{192,128},{1,193},{65,1},{129,65},{193,129... | collective-permute-start | bytes 983048 | tf_op jit(solution)/shard_map/ppermute | solution.py:160
  65.3 8.3 %collective-permute-start.8 = (bf16[320,512]{1,0:T(8,128)(2,1)S(1)}, bf16[320,512]{1,0:T(8,128)(2,1)S(1)}, u32[]{:S(2)}, u32[]{:S(2)}) collective-permute-start(bf16[320,512]{1,0:T(8,128)(2,1)S(1)} %collective-permute-done.4.ul_ref), channel_id=1, source_target_pairs={{0,64},{64,128},{128,192},{192,0},{1,65},{65,129},{129,193},{193,1... | collective-permute-start | bytes 983048 | tf_op jit(solution)/shard_map/ppermute | solution.py:162
  65.3 8.3 %collective-permute-start.9 = (bf16[320,512]{1,0:T(8,128)(2,1)S(1)}, bf16[320,512]{1,0:T(8,128)(2,1)S(1)}, u32[]{:S(2)}, u32[]{:S(2)}) collective-permute-start(bf16[320,512]{1,0:T(8,128)(2,1)S(1)} %collective-permute-done.5.dh_ref), channel_id=1, source_target_pairs={{0,192},{64,0},{128,64},{192,128},{1,193},{65,1},{129,65},{193,129... | collective-permute-start | bytes 983048 | tf_op jit(solution)/shard_map/ppermute | solution.py:163

commit v5 on v3

--- a/solution.py
+++ b/solution.py
@@ -40,7 +40,7 @@
                 out_ref[slot, s] = l_ref[s, i * SLICE : (i + 1) * SLICE, l * LANES : (l + 1) * LANES]
 
 
-def compact_kernel(pos_ref, got_ref, out_ref):
+def compact_kernel(pos_ref, _order, got_ref, out_ref):
     snodes = got_ref.shape[1]
     per_row = out_ref.shape[0] // (NX * snodes)
     count = per_row * NX * NY // (NL * NY)
@@ -185,11 +185,11 @@
     mine = pl.pallas_call(
         compact_kernel,
         out_shape=jax.ShapeDtypeStruct((blocks // NZ * snodes, SLICE, LANES), bf16),
-        in_specs=[whole(SMEM), whole()],
+        in_specs=[whole(SMEM), whole(pl.ANY), whole()],
         out_specs=whole(),
         compiler_params=params(),
         name="compact",
-    )(pos, got)
+    )(pos, block_order, got)
     half_cols = local_cols // 2
 
     def gate(own_half, after):

time: 95.2 us -> 95.2 us (level)
  no operation moved by 1% of the time
where the time goes in v5:
time: 95.2 us; the launch traced here: 94.2 us
  blocking collectives  46.4 us (49%)
  starting transfers between devices  19.6 us (21%)
  waiting for transfers between devices  13.1 us (14%)
  Pallas kernels  12.4 us (13%)
  local copies, waits for them, and re-layouts  2.48 us (3%)
    all_to_all x1, blocking collectives, per_device(): shares = lax.all_to_all(partial_value, ('l', 'y'), 0, 0, tiled=True)  17.3 us
    all_to_all x1, blocking collectives, per_device(): got = lax.all_to_all(spread, ('x', 'l', 'y'), 0, 0, tiled=True)  16.4 us
    all_to_all x1, blocking collectives, per_device(): quarters = lax.all_to_all(routed, ('l', 'y'), 0, 0, tiled=True)  12.6 us
    ppermute x1, waiting for transfers between devices, ring(): from_up = lax.ppermute(value, axis, up)  5.36 us
    pallas_call x2, Pallas kernels, gate(): pl.pallas_call(functools.partial(gate_kernel, own_half), out_shape=jax.Sh...  5.02 us
    ppermute x1, starting transfers between devices, ring(): from_up = lax.ppermute(value, axis, up)  3.35 us
    ppermute x1, starting transfers between devices, split_ring(): far_down = lax.ppermute(down_high, axis, down)  3.24 us
    ppermute x1, starting transfers between devices, split_ring(): down_low = lax.ppermute(low, axis, down)  3.23 us
  transfers between devices with their start and end apart: 10, of which 4 were waited for; matrix products, arithmetic and copies ran while one was open for 0% of the time, Pallas kernels for 8%

profile of v5, /device:TPU:32, one launch (start us, length us, event | category | flops | bytes accessed | tf_op | source)
XLA Modules:
  0.0 94.2 jit_solution(6113471708165029190)
XLA Ops:
  0.0 0.0 copy-start.1
  0.0 0.1 pad_add_fusion.pos_ref
  0.1 0.0 copy-start.3
  0.1 0.9 copy-done.3
  1.0 0.6 spread.1
  1.6 16.4 %all_to_all.19.got_ref = bf16[32,2,16,128]{3,2,1,0:T(8,128)(2,1)S(1)} all-to-all(bf16[32,2,16,128]{3,2,1,0:T(8,128)(2,1)S(1)} %spread.1), channel_id=1, replica_groups=mesh['x'=4,'z'=4,'l'=2,'y'=4,'snode'=2] {'x','l','y'}, dimensions={0} | all-to-all | bytes 524288 | tf_op jit(solution)/shard_map/all_to_all | solution.py:184
  18.0 0.0 copy-start.4
  18.1 0.7 copy-done.4
  18.7 0.6 compact.1
  19.3 3.3 %collective-permute-start = (bf16[40,16,128]{2,1,0:T(8,128)(2,1)S(1)}, bf16[40,16,128]{2,1,0:T(8,128)(2,1)S(1)}, u32[]{:S(2)}, u32[]{:S(2)}) collective-permute-start(bf16[40,16,128]{2,1,0:T(8,128)(2,1)S(1)} %compact.1), channel_id=1, source_target_pairs={{0,16},{16,32},{32,48},{48,0},{1,17},{17,33},{33,49},{49,1},{2,18}... | collective-permute-start | bytes 491528 | tf_op jit(solution)/shard_map/ppermute | solution.py:143
  22.7 2.2 %collective-permute-start.1 = (bf16[40,16,128]{2,1,0:T(8,128)(2,1)S(1)}, bf16[40,16,128]{2,1,0:T(8,128)(2,1)S(1)}, u32[]{:S(2)}, u32[]{:S(2)}) collective-permute-start(bf16[40,16,128]{2,1,0:T(8,128)(2,1)S(1)} %compact.1), channel_id=1, source_target_pairs={{0,48},{16,0},{32,16},{48,32},{1,49},{17,1},{33,17},{49,33},{2,50}... | collective-permute-start | bytes 491528 | tf_op jit(solution)/shard_map/ppermute | solution.py:144
  24.9 5.4 %collective-permute-done = bf16[40,16,128]{2,1,0:T(8,128)(2,1)S(1)} collective-permute-done((bf16[40,16,128]{2,1,0:T(8,128)(2,1)S(1)}, bf16[40,16,128]{2,1,0:T(8,128)(2,1)S(1)}, u32[]{:S(2)}, u32[]{:S(2)}) %collective-permute-start) | collective-permute-done | bytes 163872 | tf_op jit(solution)/shard_map/ppermute | solution.py:143
  30.3 1.4 %collective-permute-start.2 = (bf16[20,16,128]{2,1,0:T(8,128)(2,1)S(1)}, bf16[20,16,128]{2,1,0:T(8,128)(2,1)S(1)}, u32[]{:S(2)}, u32[]{:S(2)}) collective-permute-start(bf16[20,16,128]{2,1,0:T(8,128)(2,1)S(1)} %slice.16), channel_id=1, source_target_pairs={{0,16},{16,32},{32,48},{48,0},{1,17},{17,33},{33,49},{49,1},{2,18}... | collective-permute-start | bytes 245768 | tf_op jit(solution)/shard_map/ppermute | solution.py:145
  31.7 0.0 collective-permute-done.1
  31.7 0.0 copy-start
  31.7 0.0 copy-start.2
  31.7 2.8 %collective-permute-start.3 = (bf16[20,16,128]{2,1,0:T(8,128)(2,1)S(1)}, bf16[20,16,128]{2,1,0:T(8,128)(2,1)S(1)}, u32[]{:S(2)}, u32[]{:S(2)}) collective-permute-start(bf16[20,16,128]{2,1,0:T(8,128)(2,1)S(1)} %slice.17), channel_id=1, source_target_pairs={{0,48},{16,0},{32,16},{48,32},{1,49},{17,1},{33,17},{49,33},{2,50}... | collective-permute-start | bytes 245768 | tf_op jit(solution)/shard_map/ppermute | solution.py:146
  34.6 2.3 %collective-permute-done.2 = bf16[20,16,128]{2,1,0:T(8,128)(2,1)S(1)} collective-permute-done((bf16[20,16,128]{2,1,0:T(8,128)(2,1)S(1)}, bf16[20,16,128]{2,1,0:T(8,128)(2,1)S(1)}, u32[]{:S(2)}, u32[]{:S(2)}) %collective-permute-start.2) | collective-permute-done | bytes 81952 | tf_op jit(solution)/shard_map/ppermute | solution.py:145
  36.8 2.6 %collective-permute-done.3 = bf16[20,16,128]{2,1,0:T(8,128)(2,1)S(1)} collective-permute-done((bf16[20,16,128]{2,1,0:T(8,128)(2,1)S(1)}, bf16[20,16,128]{2,1,0:T(8,128)(2,1)S(1)}, u32[]{:S(2)}, u32[]{:S(2)}) %collective-permute-start.3) | collective-permute-done | bytes 81952 | tf_op jit(solution)/shard_map/ppermute | solution.py:146
  39.4 0.7 route.1
  40.1 12.6 %all_to_all.20 = bf16[80,2,16,128]{3,2,1,0:T(8,128)(2,1)S(1)} all-to-all(bf16[80,2,16,128]{3,2,1,0:T(8,128)(2,1)S(1)} %route.1), channel_id=1, replica_groups=mesh['x'=4,'z'=4,'l'=2,'y'=4,'snode'=2] {'l','y'}, dimensions={0} | all-to-all | bytes 1310720 | tf_op jit(solution)/shard_map/all_to_all | solution.py:218
  52.7 0.0 copy-done.1
  52.7 0.4 normal.1._after.own_ref
  53.2 0.1 collective-permute-start.4
  53.3 3.2 %collective-permute-start.5 = (bf16[320,512]{1,0:T(8,128)(2,1)S(1)}, bf16[320,512]{1,0:T(8,128)(2,1)S(1)}, u32[]{:S(2)}, u32[]{:S(2)}) collective-permute-start(bf16[320,512]{1,0:T(8,128)(2,1)S(1)} %get-tuple-element.11), channel_id=1, source_target_pairs={{0,192},{64,0},{128,64},{192,128},{1,193},{65,1},{129,65},{193,129... | collective-permute-start | bytes 983048 | tf_op jit(solution)/shard_map/ppermute | solution.py:157
  56.5 0.0 collective-permute-start.6
  56.5 3.2 %collective-permute-start.7 = (bf16[320,512]{1,0:T(8,128)(2,1)S(1)}, bf16[320,512]{1,0:T(8,128)(2,1)S(1)}, u32[]{:S(2)}, u32[]{:S(2)}) collective-permute-start(bf16[320,512]{1,0:T(8,128)(2,1)S(1)} %get-tuple-element.12), channel_id=1, source_target_pairs={{0,192},{64,0},{128,64},{192,128},{1,193},{65,1},{129,65},{193,129... | collective-permute-start | bytes 983048 | tf_op jit(solution)/shard_map/ppermute | solution.py:159
  59.7 0.0 copy-done
  59.7 0.0 copy-done.2
  59.7 2.5 %gate.2.a_ref = bf16[1280,1280]{1,0:T(8,128)(2,1)S(1)} custom-call(s32[4]{0:T(128)S(1)} %pad_add_fusion.pos_ref, s32[80,80]{1,0:T(8,128)S(1)} %copy-done.2, bf16[1280,2560]{1,0:T(8,128)(2,1)S(1)} %copy-done, bf16[640,512]{1,0:T(8,128)(2,1)S(1)} %normal.1._after.own_ref), custom_call_target="tpu_custom_call" | custom-call | flops 1638400 | bytes 6553600 | tf_op jit(solution)/shard_map/gate/pallas_call | solution.py:196
  62.3 2.9 %collective-permute-done.4.ul_ref = bf16[320,512]{1,0:T(8,128)(2,1)S(1)} collective-permute-done((bf16[320,512]{1,0:T(8,128)(2,1)S(1)}, bf16[320,512]{1,0:T(8,128)(2,1)S(1)}, u32[]{:S(2)}, u32[]{:S(2)}) %collective-permute-start.4) | collective-permute-done | bytes 327712 | tf_op jit(solution)/shard_map/ppermute | solution.py:156
  65.1 0.0 collective-permute-done.5.dh_ref
  65.1 0.0 collective-permute-start.8
  65.1 3.2 %collective-permute-start.9 = (bf16[320,512]{1,0:T(8,128)(2,1)S(1)}, bf16[320,512]{1,0:T(8,128)(2,1)S(1)}, u32[]{:S(2)}, u32[]{:S(2)}) collective-permute-start(bf16[320,512]{1,0:T(8,128)(2,1)S(1)} %collective-permute-done.5.dh_ref), channel_id=1, source_target_pairs={{0,192},{64,0},{128,64},{192,128},{1,193},{65,1},{129,65},{193,129... | collective-permute-start | bytes 983048 | tf_op jit(solution)/shard_map/ppermute | solution.py:162
  68.4 2.5 %gate.3.a_ref = bf16[1280,1280]{1,0:T(8,128)(2,1)S(1)} custom-call(s32[4]{0:T(128)S(1)} %pad_add_fusion.pos_ref, s32[80,80]{1,0:T(8,128)S(1)} %copy-done.2, bf16[1280,2560]{1,0:T(8,128)(2,1)S(1)} %copy-done, bf16[640,512]{1,0:T(8,128)(2,1)S(1)} %normal.1._after.own_ref), custom_call_target="tpu_custom_call" | custom-call | flops 1638400 | bytes 6553600 | tf_op jit(solution)/shard_map/gate/pallas_call | solution.py:196
  70.9 0.0 collective-permute-done.6.uh_ref
  70.9 0.0 collective-permute-done.7.dl_ref
  70.9 2.5 %near.1.near_ref = f32[1280,512]{1,0:T(8,128)S(1)} custom-call(s32[4]{0:T(128)S(1)} %pad_add_fusion.pos_ref, bf16[1280,1280]{1,0:T(8,128)(2,1)S(1)} %gate.3.a_ref, bf16[320,512]{1,0:T(8,128)(2,1)S(1)} %collective-permute-done.4.ul_ref, bf16[320,512]{1,0:T(8,128)(2,1)S(1)} %collective-permute-done.6.uh_ref, ...), custom_call_target="tpu_custom_call" | custom-call | flops 1677721600 | tf_op jit(solution)/shard_map/near/pallas_call | solution.py:230
  73.4 0.0 collective-permute-done.8.fu_ref
  73.4 0.0 collective-permute-done.9.fd_ref
  73.4 2.6 %far.1 = bf16[1280,512]{1,0:T(8,128)(2,1)S(1)} custom-call(s32[4]{0:T(128)S(1)} %pad_add_fusion.pos_ref, bf16[1280,1280]{1,0:T(8,128)(2,1)S(1)} %gate.2.a_ref, f32[1280,512]{1,0:T(8,128)S(1)} %near.1.near_ref, bf16[640,512]{1,0:T(8,128)(2,1)S(1)} %normal.1._after.own_ref, bf16[320,512]{1,0:T(8,128)(2,1)S(1)} %collective-permute-done.8.fu_ref, ...), custom_call_target="tpu_custom_call" | custom-call | tf_op jit(solution)/shard_map/far/pallas_call | solution.py:242
  76.0 17.3 %all_to_all.21 = bf16[8,160,512]{2,1,0:T(8,128)(2,1)S(1)} all-to-all(bf16[8,160,512]{2,1,0:T(8,128)(2,1)S(1)} %bitcast.7), channel_id=1, replica_groups=mesh['x'=4,'z'=4,'l'=2,'y'=4,'snode'=2] {'l','y'}, dimensions={0} | all-to-all | bytes 2621440 | tf_op jit(solution)/shard_map/all_to_all | solution.py:252
  93.3 0.2 reduce_sum.12
  93.5 0.7 copy.6
  (9 shorter events, 0.2 us)
Async XLA Ops:
  0.0 52.7 %copy-start.1 = (bf16[2,256,256]{2,1,0:T(8,128)(2,1)S(1)}, bf16[2,256,256]{2,1,0:T(8,128)(2,1)}, u32[]{:S(2)}) copy-start(bf16[2,256,256]{2,1,0:T(8,128)(2,1)} %diag_ref.1) | copy-start | bytes 786436
  0.1 0.9 copy-start.3
  18.0 0.7 copy-start.4
  19.3 10.9 %collective-permute-start = (bf16[40,16,128]{2,1,0:T(8,128)(2,1)S(1)}, bf16[40,16,128]{2,1,0:T(8,128)(2,1)S(1)}, u32[]{:S(2)}, u32[]{:S(2)}) collective-permute-start(bf16[40,16,128]{2,1,0:T(8,128)(2,1)S(1)} %compact.1), channel_id=1, source_target_pairs={{0,16},{16,32},{32,48},{48,0},{1,17},{17,33},{33,49},{49,1},{2,18}... | collective-permute-start | bytes 491528 | tf_op jit(solution)/shard_map/ppermute | solution.py:143
  22.7 9.0 %collective-permute-start.1 = (bf16[40,16,128]{2,1,0:T(8,128)(2,1)S(1)}, bf16[40,16,128]{2,1,0:T(8,128)(2,1)S(1)}, u32[]{:S(2)}, u32[]{:S(2)}) collective-permute-start(bf16[40,16,128]{2,1,0:T(8,128)(2,1)S(1)} %compact.1), channel_id=1, source_target_pairs={{0,48},{16,0},{32,16},{48,32},{1,49},{17,1},{33,17},{49,33},{2,50}... | collective-permute-start | bytes 491528 | tf_op jit(solution)/shard_map/ppermute | solution.py:144
  30.3 6.6 %collective-permute-start.2 = (bf16[20,16,128]{2,1,0:T(8,128)(2,1)S(1)}, bf16[20,16,128]{2,1,0:T(8,128)(2,1)S(1)}, u32[]{:S(2)}, u32[]{:S(2)}) collective-permute-start(bf16[20,16,128]{2,1,0:T(8,128)(2,1)S(1)} %slice.16), channel_id=1, source_target_pairs={{0,16},{16,32},{32,48},{48,0},{1,17},{17,33},{33,49},{49,1},{2,18}... | collective-permute-start | bytes 245768 | tf_op jit(solution)/shard_map/ppermute | solution.py:145
  31.7 28.0 %copy-start = (bf16[1280,2560]{1,0:T(8,128)(2,1)S(1)}, bf16[1280,2560]{1,0:T(8,128)(2,1)}, u32[]{:S(2)}) copy-start(bf16[1280,2560]{1,0:T(8,128)(2,1)} %a_ref.3) | copy-start | bytes 19660804
  31.7 28.0 %copy-start.2 = (s32[80,80]{1,0:T(8,128)S(1)}, s32[80,80]{1,0:T(8,128)}, u32[]{:S(2)}) copy-start(s32[80,80]{1,0:T(8,128)} %mask_ref.3) | copy-start | bytes 76804
  31.7 7.7 %collective-permute-start.3 = (bf16[20,16,128]{2,1,0:T(8,128)(2,1)S(1)}, bf16[20,16,128]{2,1,0:T(8,128)(2,1)S(1)}, u32[]{:S(2)}, u32[]{:S(2)}) collective-permute-start(bf16[20,16,128]{2,1,0:T(8,128)(2,1)S(1)} %slice.17), channel_id=1, source_target_pairs={{0,48},{16,0},{32,16},{48,32},{1,49},{17,1},{33,17},{49,33},{2,50}... | collective-permute-start | bytes 245768 | tf_op jit(solution)/shard_map/ppermute | solution.py:146
  53.2 11.9 %collective-permute-start.4 = (bf16[320,512]{1,0:T(8,128)(2,1)S(1)}, bf16[320,512]{1,0:T(8,128)(2,1)S(1)}, u32[]{:S(2)}, u32[]{:S(2)}) collective-permute-start(bf16[320,512]{1,0:T(8,128)(2,1)S(1)} %get-tuple-element.12), channel_id=1, source_target_pairs={{0,64},{64,128},{128,192},{192,0},{1,65},{65,129},{129,193},{193,1... | collective-permute-start | bytes 983048 | tf_op jit(solution)/shard_map/ppermute | solution.py:156
  53.3 11.8 %collective-permute-start.5 = (bf16[320,512]{1,0:T(8,128)(2,1)S(1)}, bf16[320,512]{1,0:T(8,128)(2,1)S(1)}, u32[]{:S(2)}, u32[]{:S(2)}) collective-permute-start(bf16[320,512]{1,0:T(8,128)(2,1)S(1)} %get-tuple-element.11), channel_id=1, source_target_pairs={{0,192},{64,0},{128,64},{192,128},{1,193},{65,1},{129,65},{193,129... | collective-permute-start | bytes 983048 | tf_op jit(solution)/shard_map/ppermute | solution.py:157
  56.5 14.4 %collective-permute-start.6 = (bf16[320,512]{1,0:T(8,128)(2,1)S(1)}, bf16[320,512]{1,0:T(8,128)(2,1)S(1)}, u32[]{:S(2)}, u32[]{:S(2)}) collective-permute-start(bf16[320,512]{1,0:T(8,128)(2,1)S(1)} %get-tuple-element.11), channel_id=1, source_target_pairs={{0,64},{64,128},{128,192},{192,0},{1,65},{65,129},{129,193},{193,1... | collective-permute-start | bytes 983048 | tf_op jit(solution)/shard_map/ppermute | solution.py:158
  56.5 14.4 %collective-permute-start.7 = (bf16[320,512]{1,0:T(8,128)(2,1)S(1)}, bf16[320,512]{1,0:T(8,128)(2,1)S(1)}, u32[]{:S(2)}, u32[]{:S(2)}) collective-permute-start(bf16[320,512]{1,0:T(8,128)(2,1)S(1)} %get-tuple-element.12), channel_id=1, source_target_pairs={{0,192},{64,0},{128,64},{192,128},{1,193},{65,1},{129,65},{193,129... | collective-permute-start | bytes 983048 | tf_op jit(solution)/shard_map/ppermute | solution.py:159
  65.1 8.3 %collective-permute-start.8 = (bf16[320,512]{1,0:T(8,128)(2,1)S(1)}, bf16[320,512]{1,0:T(8,128)(2,1)S(1)}, u32[]{:S(2)}, u32[]{:S(2)}) collective-permute-start(bf16[320,512]{1,0:T(8,128)(2,1)S(1)} %collective-permute-done.4.ul_ref), channel_id=1, source_target_pairs={{0,64},{64,128},{128,192},{192,0},{1,65},{65,129},{129,193},{193,1... | collective-permute-start | bytes 983048 | tf_op jit(solution)/shard_map/ppermute | solution.py:161
  65.1 8.3 %collective-permute-start.9 = (bf16[320,512]{1,0:T(8,128)(2,1)S(1)}, bf16[320,512]{1,0:T(8,128)(2,1)S(1)}, u32[]{:S(2)}, u32[]{:S(2)}) collective-permute-start(bf16[320,512]{1,0:T(8,128)(2,1)S(1)} %collective-permute-done.5.dh_ref), channel_id=1, source_target_pairs={{0,192},{64,0},{128,64},{192,128},{1,193},{65,1},{129,65},{193,129... | collective-permute-start | bytes 983048 | tf_op jit(solution)/shard_map/ppermute | solution.py:162
